TPU v7x, 128 devices: a whole 4x4x4 slice. The times are simulated.
128 devices in a mesh: expert: 32 (over z, x, core), mp: 4 (over y).
Axes of the slice: x: 4, y: 4, z: 4, core: 2. Of those that a mesh axis runs over, the one named last changes fastest.
Arguments:
- tokens: bfloat16 [16384, 1024], P(('expert', 'mp')), may hold values from -6 to 6
- out_grad: bfloat16 [16384, 1024], P(('expert', 'mp')), may hold values from -6 to 6
- routes: int32 [16384, 8], P('expert'), may hold values from 0 to 63, all different within a row; in each aligned block of 512 rows (0 to 511, 512 to 1023, ...) at most 80 rows name the same one
- gates: float32 [16384, 8], P('expert'), may hold values from 0.05 to 0.4
- w_gate: bfloat16 [64, 1024, 1024], P('expert', None, 'mp'), may hold values from -0.1875 to 0.1875
- w_up: bfloat16 [64, 1024, 1024], P('expert', None, 'mp'), may hold values from -0.1875 to 0.1875
- w_down: bfloat16 [64, 1024, 1024], P('expert', 'mp'), may hold values from -0.1875 to 0.1875
Outputs:
- grad_tokens: bfloat16 [16384, 1024], P(('expert', 'mp'))
- grad_gate: float32 [64, 1024, 1024], P('expert', None, 'mp')
- grad_up: float32 [64, 1024, 1024], P('expert', None, 'mp')
- grad_down: float32 [64, 1024, 1024], P('expert', 'mp')
Inputs may be any that keep to these rules, and one draw needn't show every extreme that they name: `routes`: each row names 8 different experts. Within each aligned block of 512 rows (the rows of one index of expert) no expert is named by more than 80 rows, a bound that some block reaches.
All inputs are finite; a program needn't handle non-finite values.
Results may differ from a plain program's by a relative error of at most 0.017.
Values may be sent and summed in bfloat16 or wider, within the bound.
A program may use at most 192 MiB of HBM per device.

v0:
```python
import jax
import jax.numpy as jnp
from jax import lax
from jax.sharding import PartitionSpec as P


def shards(tokens, out_grad, routes, gates, w_gate, w_up, w_down):
    n_mp = lax.axis_size("mp")
    n_expert = lax.axis_size("expert")
    local_experts = w_gate.shape[0]
    experts = local_experts * n_expert
    group_tok, topk = routes.shape
    width = tokens.shape[1]
    capacity = n_mp * (group_tok * topk * 5 // (4 * experts * n_mp))
    route_count = group_tok * topk
    group_x, group_dy = (
        lax.all_gather(tokens, "mp", axis=0, tiled=True),
        lax.all_gather(out_grad, "mp", axis=0, tiled=True),
    )
    flat = routes.reshape(-1)
    expert_ids = jnp.arange(experts, dtype=jnp.int32)
    onehot = (flat[:, None] == expert_ids[None, :]).astype(jnp.int32)
    before = jnp.sum((jnp.cumsum(onehot, axis=0) - onehot) * onehot, axis=1)
    slot = flat * capacity + before
    owner = (
        jnp.full((experts * capacity,), route_count, jnp.int32)
        .at[slot]
        .set(jnp.arange(route_count, dtype=jnp.int32))
    )
    token_rows = owner // topk
    x_pad = jnp.concatenate([group_x, jnp.zeros((1, width), jnp.bfloat16)], axis=0)
    dy_pad = jnp.concatenate([group_dy, jnp.zeros((1, width), jnp.bfloat16)], axis=0)
    gate_pad = jnp.concatenate([gates.reshape(-1), jnp.zeros((1,), jnp.float32)], axis=0)
    send_x = x_pad[token_rows].reshape(n_expert, local_experts, capacity, width)
    send_dy = (gate_pad[owner][:, None] * dy_pad[token_rows].astype(jnp.float32)).astype(
        jnp.bfloat16
    )
    send_dy = send_dy.reshape(n_expert, local_experts, capacity, width)
    recv_x, recv_dy = (
        lax.all_to_all(send_x, "expert", split_axis=0, concat_axis=0, tiled=True),
        lax.all_to_all(send_dy, "expert", split_axis=0, concat_axis=0, tiled=True),
    )
    pre_gate = jnp.einsum("secd,edf->secf", recv_x, w_gate, preferred_element_type=jnp.float32)
    pre_up = jnp.einsum("secd,edf->secf", recv_x, w_up, preferred_element_type=jnp.float32)
    sig = jax.nn.sigmoid(pre_gate)
    hidden = (pre_gate * sig * pre_up).astype(jnp.bfloat16)
    d_hidden = jnp.einsum("secd,efd->secf", recv_dy, w_down, preferred_element_type=jnp.float32)
    grad_down = jnp.einsum("secf,secd->efd", hidden, recv_dy, preferred_element_type=jnp.float32)
    d_up = (d_hidden * pre_gate * sig).astype(jnp.bfloat16)
    d_gate = (d_hidden * pre_up * sig * (1.0 + pre_gate * (1.0 - sig))).astype(jnp.bfloat16)
    grad_gate = jnp.einsum("secd,secf->edf", recv_x, d_gate, preferred_element_type=jnp.float32)
    grad_up = jnp.einsum("secd,secf->edf", recv_x, d_up, preferred_element_type=jnp.float32)
    part = jnp.einsum("secf,edf->secd", d_gate, w_gate, preferred_element_type=jnp.float32)
    part = part + jnp.einsum("secf,edf->secd", d_up, w_up, preferred_element_type=jnp.float32)
    part = part.astype(jnp.bfloat16)
    back = lax.all_to_all(part, "expert", split_axis=0, concat_axis=0, tiled=True)
    rows = back.reshape(experts * capacity, width)[slot].astype(jnp.float32)
    group_dx = jnp.sum(rows.reshape(group_tok, topk, width), axis=1)
    grad_tokens = lax.psum_scatter(
        group_dx.astype(jnp.bfloat16), "mp", scatter_dimension=0, tiled=True
    )
    return (grad_tokens, grad_gate, grad_up, grad_down)


def solution(mesh):
    in_specs = (
        P(("expert", "mp"), None),
        P(("expert", "mp"), None),
        P("expert", None),
        P("expert", None),
        P("expert", None, "mp"),
        P("expert", None, "mp"),
        P("expert", "mp", None),
    )
    out_specs = (
        P(("expert", "mp"), None),
        P("expert", None, "mp"),
        P("expert", None, "mp"),
        P("expert", "mp", None),
    )
    return jax.shard_map(shards, mesh=mesh, in_specs=in_specs, out_specs=out_specs, check_vma=False)
```

profile of v0, /device:TPU:0, one launch (start us, length us, event | category | flops | bytes accessed | tf_op | source)
XLA Modules:
  0.0 599.5 jit_solution(12219961693879175144)
XLA Ops:
  7.2 0.0 all-gather.5.cloned.1.call-start
  7.2 0.7 all-gather.5.cloned.1.call-update
  7.9 0.7 broadcast_multiply_fusion
  8.6 0.8 copy.23
  9.5 0.1 eq.29
  9.6 0.1 eq.25
  9.8 0.1 copy.22
  9.9 0.2 mul.56
  10.1 0.1 fusion.47
  10.2 18.4 %reduce-window.6 = s32[64,32,128]{2,1,0:T(8,128)S(1)} reduce-window(s32[64,32,128]{2,1,0:T(8,128)S(1)} %fusion.47, s32[]{:T(128)} %constant.16.clone.1), window={size=1x1x128 pad=0_0x0_0x127_0}, to_apply=%region_0.0 | reduce-window | flops 33292288 | bytes 2097156 | tf_op jit(solution)/shard_map/reduce-window
  28.7 0.3 slice.16
  29.0 0.4 copy.42
  29.4 0.2 reduce-window.9
  29.6 0.3 broadcast_add_fusion
  30.0 0.9 fusion.40
  30.9 15.5 %scatter_custom_fusion = s32[5120]{0:T(1024)S(1)} fusion(s32[4096]{0:T(1024)S(1)} %bitcast.116, s32[4096]{0:T(1024)S(1)} %iota.11, s32[]{:T(128)} %constant.12.clone.1), kind=kCustom, calls=%fused_computation.69 | custom fusion | bytes 20484 | tf_op jit(solution)/shard_map/scatter | solution.py:28
  46.5 0.0 all-gather.5.cloned.1.call-done
  46.5 1.3 concatenate.11
  47.8 22.5 %gather_fusion.2 = bf16[5120,1024]{1,0:T(8,128)(2,1)} fusion(bf16[513,1024]{1,0:T(8,128)(2,1)S(1)} %concatenate.11, s32[5120]{0:T(1024)S(1)} %get-tuple-element.7), kind=kCustom, calls=%fused_computation.2 | custom fusion | bytes 20992000 | tf_op jit(solution)/shard_map/gather | solution.py:34
  70.4 8.5 %all-to-all-start.1 = ((bf16[32,2,80,1024]{3,2,1,0:T(8,128)(2,1)}), bf16[32,2,80,1024]{3,2,1,0:T(8,128)(2,1)}, u32[]{:S(2)}, u32[]{:S(2)}) async-start(bf16[32,2,80,1024]{3,2,1,0:T(8,128)(2,1)} %bitcast.110), calls=%async_computation.1 | async-start | bytes 20971520 | tf_op jit(solution)/shard_map/all_to_all | solution.py:40
  78.9 0.0 all-gather.3.cloned.1.call-start
  78.9 0.7 all-gather.3.cloned.1.call-update
  79.7 0.1 copy.21
  79.8 0.2 reshape.75
  79.9 28.7 %gather_fusion = f32[5120]{0:T(1024)S(1)} fusion(f32[4097]{0:T(1024)S(1)} %pad_maximum_fusion, s32[5120]{0:T(1024)S(1)} %get-tuple-element.6), kind=kCustom, calls=%fused_computation | custom fusion | bytes 61440 | tf_op jit(solution)/shard_map/gather | solution.py:35
  108.6 0.1 mul.58
  108.7 0.0 all-gather.3.cloned.1.call-done
  108.8 1.3 concatenate.10
  110.1 22.5 %gather_fusion.1 = bf16[5120,1024]{1,0:T(8,128)(2,1)} fusion(bf16[513,1024]{1,0:T(8,128)(2,1)S(1)} %concatenate.10, s32[5120]{0:T(1024)S(1)} %get-tuple-element.7), kind=kCustom, calls=%fused_computation.1 | custom fusion | bytes 20992000 | tf_op jit(solution)/shard_map/gather | solution.py:35
  132.5 10.5 %fusion = bf16[32,2,80,1024]{3,2,1,0:T(8,128)(2,1)} fusion(bf16[32,2,80,1024]{3,2,1,0:T(8,128)(2,1)} %bitcast.111, f32[32,2,80]{2,1,0:T(2,128)S(1)} %mul.58), kind=kLoop, calls=%fused_computation.6 | loop fusion | flops 15728640 | bytes 20992000 | tf_op jit(solution)/shard_map/convert_element_type | solution.py:35
  143.0 68.6 %all-to-all-done.1 = bf16[32,2,80,1024]{3,2,1,0:T(8,128)(2,1)} async-done(((bf16[32,2,80,1024]{3,2,1,0:T(8,128)(2,1)}), bf16[32,2,80,1024]{3,2,1,0:T(8,128)(2,1)}, u32[]{:S(2)}, u32[]{:S(2)}) %all-to-all-start.1) | async-done | bytes 10485792 | tf_op jit(solution)/shard_map/all_to_all | solution.py:40
  211.6 5.3 all-to-all-start
  216.9 9.2 %fusion.4 = f32[2,32,80,256]{3,2,1,0:T(8,128)} fusion(bf16[32,2,80,1024]{3,2,1,0:T(8,128)(2,1)} %all-to-all-done.1, bf16[2,1024,256]{2,1,0:T(8,128)(2,1)S(1)} %copy-done.3), kind=kOutput, calls=%fused_computation.11 | convolution fusion | flops 2684354560 | bytes 16777216 | tf_op jit(solution)/shard_map/secd,edf->secf/dot_general | solution.py:44
  226.2 123.4 %all-to-all-done = bf16[32,2,80,1024]{3,2,1,0:T(8,128)(2,1)} async-done(((bf16[32,2,80,1024]{3,2,1,0:T(8,128)(2,1)}), bf16[32,2,80,1024]{3,2,1,0:T(8,128)(2,1)}, u32[]{:S(2)}, u32[]{:S(2)}) %all-to-all-start) | async-done | bytes 10485792 | tf_op jit(solution)/shard_map/all_to_all | solution.py:41
  349.6 6.0 fusion.8
  355.6 9.2 %fusion.17 = (bf16[32,2,80,256]{3,2,0,1:T(8,128)(2,1)}, bf16[32,2,80,256]{3,2,0,1:T(8,128)(2,1)S(1)}, f32[2,32,80,256]{3,2,1,0:T(8,128)}) fusion(f32[2,32,80,256]{3,2,1,0:T(8,128)S(1)} %fusion.8, f32[2,32,80,256]{3,2,1,0:T(8,128)S(1)} %copy-done.6, bf16[2,1024,256]{2,1,0:T(8,128)(2,1)S(1)} %copy-done, bf16[32,2,80,1024]{3,2,1,0:T(8,128)(2,1)} %all-to-all-done.1), kind=kOutput, calls=%fused_computation.29 | convolution fusion | flops 2701393920 | bytes 32505856 | tf_op jit(solution)/shard_map/secd,edf->secf/dot_general | solution.py:43
  364.8 8.5 %fusion.41 = f32[2,32,80,1024]{3,2,1,0:T(8,128)} fusion(bf16[32,2,80,256]{3,2,0,1:T(8,128)(2,1)S(1)} %get-tuple-element.5, bf16[2,1024,256]{2,1,0:T(8,128)(2,1)S(1)} %copy-done), kind=kOutput, calls=%fused_computation.46 | convolution fusion | flops 2684354560 | bytes 24641536 | tf_op jit(solution)/shard_map/secf,edf->secd/dot_general | solution.py:53
  373.3 12.6 %fusion.1 = bf16[32,2,80,1024]{3,2,0,1:T(8,128)(2,1)} fusion(f32[2,32,80,1024]{3,2,1,0:T(8,128)} %fusion.41, bf16[32,2,80,256]{3,2,0,1:T(8,128)(2,1)} %get-tuple-element.4, bf16[2,1024,256]{2,1,0:T(8,128)(2,1)S(1)} %copy-done.3), kind=kOutput, calls=%fused_computation.8 | convolution fusion | flops 2694840320 | bytes 35127296 | tf_op jit(solution)/shard_map/secf,edf->secd/dot_general | solution.py:54
  385.9 10.1 %copy.30 = bf16[32,2,80,1024]{3,2,1,0:T(8,128)(2,1)} copy(bf16[32,2,80,1024]{3,2,0,1:T(8,128)(2,1)} %fusion.1) | data formatting | bytes 20971520 | tf_op jit(solution)/shard_map/convert_element_type | solution.py:55
  396.1 5.0 all-to-all-start.2
  401.1 12.4 %reduce-scatter.2.cloned.1.call-start = ((), (), s32[]{:S(2)}) async-start(), calls=%async_computation.6 | async-start | bytes 1310720 | tf_op jit(solution)/shard_map/reduce_scatter | solution.py:59
  413.5 10.2 %fusion.30 = f32[2,1024,256]{2,1,0:T(8,128)} fusion(bf16[32,2,80,1024]{3,2,1,0:T(8,128)(2,1)} %all-to-all-done.1, bf16[32,2,80,256]{3,2,0,1:T(8,128)(2,1)} %get-tuple-element.4), kind=kOutput, calls=%fused_computation.40 | convolution fusion | flops 2684354560 | bytes 15204352 | tf_op jit(solution)/shard_map/secd,secf->edf/dot_general | solution.py:52
  423.7 110.2 %all-to-all-done.2 = bf16[32,2,80,1024]{3,2,1,0:T(8,128)(2,1)} async-done(((bf16[32,2,80,1024]{3,2,1,0:T(8,128)(2,1)}), bf16[32,2,80,1024]{3,2,1,0:T(8,128)(2,1)}, u32[]{:S(2)}, u32[]{:S(2)}) %all-to-all-start.2) | async-done | bytes 10485792 | tf_op jit(solution)/shard_map/all_to_all | solution.py:56
  533.9 26.1 %gather_fusion.3 = bf16[4096,1024]{1,0:T(8,128)(2,1)} fusion(bf16[5120,1024]{1,0:T(8,128)(2,1)} %bitcast.18, s32[4096]{0:T(1024)S(1)} %broadcast_clamp_fusion), kind=kCustom, calls=%fused_computation.3 | custom fusion | bytes 16793600 | tf_op jit(solution)/shard_map/gather | solution.py:57
  560.0 11.7 %bitcast_reduce_fusion = bf16[512,1024]{1,0:T(8,128)(2,1)} fusion(bf16[4096,1024]{1,0:T(8,128)(2,1)} %gather_fusion.3), kind=kLoop, calls=%fused_computation.17 | loop fusion | flops 3670016 | bytes 9437184 | tf_op jit(solution)/shard_map/reduce_sum | solution.py:58
  571.7 0.0 reduce-scatter.2.cloned.1.call-update
  571.8 10.4 %fusion.27 = f32[2,1024,256]{2,1,0:T(8,128)} fusion(bf16[32,2,80,1024]{3,2,1,0:T(8,128)(2,1)} %all-to-all-done.1, bf16[32,2,80,256]{3,2,0,1:T(8,128)(2,1)} %copy-done.2), kind=kOutput, calls=%fused_computation.39 | convolution fusion | flops 2684354560 | bytes 15204352 | tf_op jit(solution)/shard_map/secd,secf->edf/dot_general | solution.py:51
  582.1 10.6 %fusion.33 = f32[2,256,1024]{2,1,0:T(8,128)} fusion(bf16[32,2,80,1024]{3,2,1,0:T(8,128)(2,1)} %all-to-all-done, f32[2,32,80,256]{3,2,1,0:T(8,128)} %get-tuple-element.8, f32[2,32,80,256]{3,2,1,0:T(8,128)S(1)} %bitcast.119), kind=kOutput, calls=%fused_computation.41 | convolution fusion | flops 2692218880 | bytes 23068672 | tf_op jit(solution)/shard_map/secf,secd->efd/dot_general | solution.py:48
  (25 shorter events, 0.1 us)
Async XLA Ops:
  7.2 348.4 %copy-start = (bf16[2,1024,256]{2,1,0:T(8,128)(2,1)S(1)}, bf16[2,1024,256]{2,1,0:T(8,128)(2,1)}, u32[]{:S(2)}) copy-start(bf16[2,1024,256]{2,1,0:T(8,128)(2,1)} %param.11) | copy-start | bytes 3145732
  7.2 39.4 %all-gather.5.cloned.1.call-start = ((), (), s32[]{:S(2)}) async-start(), calls=%async_computation.5 | async-start | bytes 1310720 | tf_op jit(solution)/shard_map/all_gather | solution.py:17
  70.4 9.3 %copy-start.4 = (f32[512,8]{0,1:T(8,128)S(1)}, f32[512,8]{0,1:T(8,128)}, u32[]{:S(2)}) copy-start(f32[512,8]{0,1:T(8,128)} %param.10) | copy-start | bytes 49156
  70.4 141.2 %all-to-all-start.1 = ((bf16[32,2,80,1024]{3,2,1,0:T(8,128)(2,1)}), bf16[32,2,80,1024]{3,2,1,0:T(8,128)(2,1)}, u32[]{:S(2)}, u32[]{:S(2)}) async-start(bf16[32,2,80,1024]{3,2,1,0:T(8,128)(2,1)} %bitcast.110), calls=%async_computation.1 | async-start | bytes 20971520 | tf_op jit(solution)/shard_map/all_to_all | solution.py:40
  78.9 29.9 %all-gather.3.cloned.1.call-start = ((), (), s32[]{:S(2)}) async-start(), calls=%async_computation.4 | async-start | bytes 1310720 | tf_op jit(solution)/shard_map/all_gather | solution.py:18
  143.0 73.9 %copy-start.3 = (bf16[2,1024,256]{2,1,0:T(8,128)(2,1)S(1)}, bf16[2,1024,256]{2,1,0:T(8,128)(2,1)}, u32[]{:S(2)}) copy-start(bf16[2,1024,256]{2,1,0:T(8,128)(2,1)} %param.12) | copy-start | bytes 3145732
  211.6 137.9 %all-to-all-start = ((bf16[32,2,80,1024]{3,2,1,0:T(8,128)(2,1)}), bf16[32,2,80,1024]{3,2,1,0:T(8,128)(2,1)}, u32[]{:S(2)}, u32[]{:S(2)}) async-start(bf16[32,2,80,1024]{3,2,1,0:T(8,128)(2,1)} %fusion), calls=%async_computation | async-start | bytes 20971520 | tf_op jit(solution)/shard_map/all_to_all | solution.py:41
  216.9 132.7 %copy-start.5 = (bf16[2,256,1024]{2,1,0:T(8,128)(2,1)S(1)}, bf16[2,256,1024]{2,1,0:T(8,128)(2,1)}, u32[]{:S(2)}) copy-start(bf16[2,256,1024]{2,1,0:T(8,128)(2,1)} %param.13) | copy-start | bytes 3145732
  349.6 6.0 %copy-start.6 = (f32[2,32,80,256]{3,2,1,0:T(8,128)S(1)}, f32[2,32,80,256]{3,2,1,0:T(8,128)}, u32[]{:S(2)}) copy-start(f32[2,32,80,256]{3,2,1,0:T(8,128)} %fusion.4) | copy-start | bytes 15728644
  364.8 8.5 %copy-start.2 = (bf16[32,2,80,256]{3,2,0,1:T(8,128)(2,1)}, bf16[32,2,80,256]{3,2,0,1:T(8,128)(2,1)S(1)}, u32[]{:S(2)}) copy-start(bf16[32,2,80,256]{3,2,0,1:T(8,128)(2,1)S(1)} %get-tuple-element.5) | copy-start | bytes 7864324
  396.1 137.8 %all-to-all-start.2 = ((bf16[32,2,80,1024]{3,2,1,0:T(8,128)(2,1)}), bf16[32,2,80,1024]{3,2,1,0:T(8,128)(2,1)}, u32[]{:S(2)}, u32[]{:S(2)}) async-start(bf16[32,2,80,1024]{3,2,1,0:T(8,128)(2,1)} %copy.30), calls=%async_computation.2 | async-start | bytes 20971520 | tf_op jit(solution)/shard_map/all_to_all | solution.py:56
  401.1 191.6 %reduce-scatter.2.cloned.1.call-start = ((), (), s32[]{:S(2)}) async-start(), calls=%async_computation.6 | async-start | bytes 1310720 | tf_op jit(solution)/shard_map/reduce_scatter | solution.py:59
  560.0 22.1 %slice-start = ((s8[5242880]{0:T(1024)(128)(4,1)}), s8[1048576]{0:T(1024)(128)(4,1)S(1)}, s32[]{:S(2)}) async-start(s8[5242880]{0:T(1024)(128)(4,1)} %bitcast.118), calls=%async_computation.7 | async-start | bytes 2097152
  571.8 10.4 %slice-start.1 = ((s8[5242880]{0:T(1024)(128)(4,1)}), s8[4194304]{0:T(1024)(128)(4,1)S(1)}, s32[]{:S(2)}) async-start(s8[5242880]{0:T(1024)(128)(4,1)} %bitcast.118), calls=%async_computation.8 | async-start | bytes 8388608
  582.1 10.6 %copy-start.1 = (bf16[2,1024,256]{2,1,0:T(8,128)(2,1)S(1)}, bf16[2,1024,256]{2,1,0:T(8,128)(2,1)}, u32[]{:S(2)}) copy-start(bf16[2,1024,256]{2,1,0:T(8,128)(2,1)} %param.11) | copy-start | bytes 3145732
Sparse Core Ops, SparseCore 0:
  9.7 26.4 all-gather.4
  81.4 25.5 all-gather.2
  571.9 20.3 reduce-scatter.1
where the time goes:
time: 605 us; the launch traced here: 599 us
  waiting for transfers between devices  304 us (50%)
  local copies, waits for them, and re-layouts  131 us (22%)
  matrix products  76.7 us (13%)
  other arithmetic  43 us (7%)
  starting transfers between devices  31.3 us (5%)
  between operations  14.2 us (2%)
    all_to_all x1, waiting for transfers between devices, shards(): lax.all_to_all(send_dy, 'expert', split_axis=0, concat_axis=0, tiled=True)  123 us
    all_to_all x1, waiting for transfers between devices, shards(): lax.all_to_all(part, 'expert', split_axis=0, concat_axis=0, tiled=True)  110 us
    all_to_all x1, waiting for transfers between devices, shards(): lax.all_to_all(send_x, 'expert', split_axis=0, concat_axis=0, tiled=True)  68.6 us
    gather x1, local copies, waits for them, and re-layouts, shards(): gate_pad[owner][:, None] * dy_pad[token_rows].astype(jnp.float32)  28.7 us
    gather x1, local copies, waits for them, and re-layouts, shards(): rows = back.reshape(experts * capacity, width)[slot].astype(jnp.float32)  26.1 us
    gather x1, local copies, waits for them, and re-layouts, shards(): send_x = x_pad[token_rows].reshape(n_expert, local_experts, capacity, width)  22.5 us
    gather x1, local copies, waits for them, and re-layouts, shards(): dy_pad[token_rows].astype(jnp.float32)  22.5 us
    another operation x3, other arithmetic  19 us
  transfers between devices with their start and end apart: 6, of which 3 were waited for; matrix products, arithmetic and copies ran while one was open for 24% of the time, Pallas kernels for 0%

commit v1 on v0

v1 whole, which is shorter than its diff:
```python
import jax
import jax.numpy as jnp
from jax import lax
from jax.experimental import pallas as pl
from jax.experimental.pallas import tpu as pltpu
from jax.sharding import PartitionSpec as P

MESH = pl.DeviceIdType.MESH
BF16, F32 = jnp.bfloat16, jnp.float32
TOK, TILES, LANES = 128, 8, 128
CAP = 80
META = TILES * 2 * TOK
MROWS = META + 32
SPLIT = ((0, 688), (688, 688), (1376, 704))
BACK = ((0, 336), (336, 336), (672, 352))
ORDER = ((0, 1, 2), (1, 2, 0), (2, 0, 1))


def where_am_i():
    e = lax.axis_index("expert")
    return (e // 8, (e // 2) % 4, lax.axis_index("mp")), e % 2


def dev_of(pos, core):
    return ((pos[0] * 4 + pos[1]) * 2 + core, pos[2])


def index_of(pos, core):
    return ((pos[0] * 4 + pos[1]) * 2 + core) * 4 + pos[2]


def lin(pos):
    return (pos[0] * 4 + pos[1]) * 4 + pos[2]


def moved(pos, axis, by):
    p = list(pos)
    p[axis] = (p[axis] + by + 4) % 4
    return tuple(p)


def rows_of(split, r, half):
    start, size = split[r]
    low = (size // 32) * 16
    if half is None:
        return start, size
    return (start, low) if half == 0 else (start + low, size - low)


def greet(me, core):
    barrier = pltpu.get_barrier_semaphore()
    for axis in range(3):
        for d in (1, -1):
            pl.semaphore_signal(barrier, inc=1, device_id=dev_of(moved(me, axis, d), core), device_id_type=MESH)
    pl.semaphore_signal(barrier, inc=1, device_id=dev_of(me, 1 - core), device_id_type=MESH)
    pl.semaphore_wait(barrier, 7)


def gather_kernel(msg, buf, send_sem, recv_sem, pair_send, pair_recv, own_sem):
    me, core = where_am_i()
    other = dev_of(me, 1 - core)
    greet(me, core)
    own = pltpu.make_async_copy(msg, buf.at[index_of(me, core)], own_sem)
    own.start()

    def ring(r, pos, half, axis, d, mine=False):
        start, size = rows_of(SPLIT, r, half)
        idx = index_of(pos, core)
        src = msg if mine else buf.at[idx]
        return pltpu.make_async_remote_copy(
            src_ref=src.at[pl.ds(start, size)], dst_ref=buf.at[idx, pl.ds(start, size)],
            send_sem=send_sem, recv_sem=recv_sem.at[r, lin(pos), 0 if half is None else half],
            device_id=dev_of(moved(me, axis, d), core), device_id_type=MESH)

    def pair(r, pos, mine=False):
        start, size = SPLIT[r]
        idx = index_of(pos, core)
        src = msg if mine else buf.at[idx]
        pltpu.make_async_remote_copy(
            src_ref=src.at[pl.ds(start, size)], dst_ref=buf.at[idx, pl.ds(start, size)],
            send_sem=pair_send, recv_sem=pair_recv,
            device_id=other, device_id_type=MESH).start()

    def send_full(r, pos, phase, mine=False):
        for p in range(phase, 3):
            for d in (1, -1):
                ring(r, pos, None, ORDER[r][p], d, mine).start()

    def near(r, base, phase):
        axis = ORDER[r][phase]
        for d in (1, -1):
            pos = moved(base, axis, -d)
            ring(r, pos, None, axis, d).wait_recv()
            ring(r, pos, 0 if d == 1 else 1, axis, d).start()
            pair(r, pos)
            send_full(r, pos, phase + 1)

    def far(r, base, phase):
        axis = ORDER[r][phase]
        pos = moved(base, axis, 2)
        for half in (0, 1):
            ring(r, pos, half, axis, 1).wait_recv()
        pair(r, pos)
        send_full(r, pos, phase + 1)

    for r in range(3):
        send_full(r, me, 0, mine=True)
    for r in range(3):
        pair(r, me, mine=True)
    for step in (near, far):
        for r in range(3):
            step(r, me, 0)
    for step in (near, far):
        def line(i, c, step=step):
            for r in range(3):
                step(r, moved(me, ORDER[r][0], i), 1)
            return c
        lax.fori_loop(0, 4, line, 0)
    for step in (near, far):
        def plane(i, c, step=step):
            for r in range(3):
                step(r, moved(moved(me, ORDER[r][0], i // 4), ORDER[r][1], i % 4), 2)
            return c
        lax.fori_loop(0, 16, plane, 0)
    own.wait()
    half = buf.at[pl.ds(0, 64)]
    pltpu.make_async_copy(half, half, pair_recv).wait()
    pltpu.make_async_copy(half, half, pair_send).wait()
    most = buf.at[pl.ds(0, 63)]
    pltpu.make_async_copy(most, most, send_sem).wait()


def gather_all(msg):
    dma = pltpu.SemaphoreType.DMA
    return pl.pallas_call(
        gather_kernel,
        out_shape=jax.ShapeDtypeStruct((128, MROWS, LANES), BF16),
        in_specs=[pl.BlockSpec(memory_space=pl.ANY)],
        out_specs=pl.BlockSpec(memory_space=pl.ANY),
        scratch_shapes=[dma, dma((3, 64, 2)), dma, dma, dma],
        compiler_params=pltpu.CompilerParams(collective_id=0, has_side_effects=True),
    )(msg)


def tn(a, b):
    return lax.dot_general(a, b, (((0,), (0,)), ((), ())), preferred_element_type=F32)


def nt(a, b):
    return lax.dot_general(a, b, (((1,), (1,)), ((), ())), preferred_element_type=F32)


BLOCKS = 4


def expert_kernel(buf, wg, wu, wd, partial, gg, gu, gd, xs, ss, ps, part):
    step = pl.program_id(0)
    first = lax.axis_index("expert") * 2

    @pl.when(step == 0)
    def _():
        gg[...] = jnp.zeros_like(gg)
        gu[...] = jnp.zeros_like(gu)
        gd[...] = jnp.zeros_like(gd)

    slots = lax.broadcasted_iota(jnp.int32, (CAP, TOK), 0).astype(F32)

    def pick(b, c):
        hots, gates = [[], []], [0.0, 0.0]
        for y in range(4):
            meta = buf[b * 4 + y, pl.ds(META, 32), :].astype(F32)
            for j in range(2):
                named = (meta[0:8] == (first + j).astype(F32)).astype(F32)
                at = jnp.sum(named * (meta[8:16] + 1.0), axis=0, keepdims=True) - 1.0
                gate = jnp.sum(named * (meta[16:24] + meta[24:32]), axis=0, keepdims=True)
                hot = (slots == at).astype(F32)
                hots[j].append(hot)
                gates[j] = gates[j] + jnp.sum(hot * gate, axis=1, keepdims=True)
        hot = jnp.concatenate([jnp.concatenate(h, axis=1) for h in hots], axis=0).astype(BF16)
        gate = jnp.concatenate(gates, axis=0)
        ps[b] = hot
        for t in range(0, TILES, 2):
            def cols(at):
                return jnp.concatenate([
                    jnp.concatenate([buf[b * 4 + y, pl.ds((t + u) * 2 * TOK + at, TOK), :] for u in range(2)], axis=1)
                    for y in range(4)], axis=0)
            x = jnp.dot(hot, cols(0), preferred_element_type=F32).astype(BF16)
            s = (gate * jnp.dot(hot, cols(TOK), preferred_element_type=F32)).astype(BF16)
            for j in range(2):
                rows = pl.ds(pl.multiple_of(b * CAP, 16), CAP)
                xs[j, rows, pl.ds(t * LANES, 2 * LANES)] = x[j * CAP:(j + 1) * CAP]
                ss[j, rows, pl.ds(t * LANES, 2 * LANES)] = s[j * CAP:(j + 1) * CAP]
        return c

    lax.fori_loop(0, BLOCKS, pick, 0)
    for j in range(2):
        x, s = xs[j], ss[j]
        pre_gate = jnp.dot(x, wg[j], preferred_element_type=F32)
        pre_up = jnp.dot(x, wu[j], preferred_element_type=F32)
        d_hidden = nt(s, wd[j])
        sig = jax.nn.sigmoid(pre_gate)
        act = pre_gate * sig
        hidden = (act * pre_up).astype(BF16)
        d_up = (d_hidden * act).astype(BF16)
        d_gate = (d_hidden * pre_up * sig * (1.0 + pre_gate * (1.0 - sig))).astype(BF16)
        gd[j] += tn(hidden, s)
        gg[j] += tn(x, d_gate)
        gu[j] += tn(x, d_up)
        part[j] = (nt(d_gate, wg[j]) + nt(d_up, wu[j])).astype(BF16)

    def place(b, c):
        hot = ps[b]
        rows = pl.ds(pl.multiple_of(b * CAP, 16), CAP)
        for t in range(0, TILES, 2):
            both = jnp.concatenate([part[j, rows, pl.ds(t * LANES, 2 * LANES)] for j in range(2)], axis=0)
            out = tn(hot, both).astype(BF16)
            for y in range(4):
                for u in range(2):
                    partial[b * 4 + y, pl.ds((t + u) * TOK, TOK), :] = out[y * TOK:(y + 1) * TOK, u * LANES:(u + 1) * LANES]
        return c

    lax.fori_loop(0, BLOCKS, place, 0)


def experts(buf, wg, wu, wd):
    whole = lambda a: pl.BlockSpec(a.shape, lambda i: (0, 0, 0), pipeline_mode=pl.Buffered(1))
    g = jax.ShapeDtypeStruct(wg.shape, F32)
    d = jax.ShapeDtypeStruct(wd.shape, F32)
    n = BLOCKS * 4
    return pl.pallas_call(
        expert_kernel,
        grid=(128 // n,),
        out_shape=(jax.ShapeDtypeStruct((128, TILES * TOK, LANES), BF16), g, g, d),
        in_specs=[pl.BlockSpec((n, MROWS, LANES), lambda i: (i, 0, 0)), whole(wg), whole(wu), whole(wd)],
        out_specs=(pl.BlockSpec((n, TILES * TOK, LANES), lambda i: (i, 0, 0)), whole(g), whole(g), whole(d)),
        scratch_shapes=[pltpu.VMEM((2, BLOCKS * CAP, 1024), BF16), pltpu.VMEM((2, BLOCKS * CAP, 1024), BF16),
                        pltpu.VMEM((BLOCKS, 2 * CAP, 512), BF16), pltpu.VMEM((2, BLOCKS * CAP, 1024), BF16)],
        compiler_params=pltpu.CompilerParams(vmem_limit_bytes=60 * 1024 * 1024),
    )(buf, wg, wu, wd)


def scatter_kernel(partial, out, mine, theirs, land, send_sem, recv_sem, pair_send, pair_recv, load_sem, out_sem):
    me, core = where_am_i()
    other = dev_of(me, 1 - core)
    greet(me, core)

    def pair(r, pos):
        start, size = BACK[r]
        return pltpu.make_async_remote_copy(
            src_ref=partial.at[index_of(pos, 1 - core), pl.ds(start, size)],
            dst_ref=theirs.at[lin(pos), pl.ds(start, size)],
            send_sem=pair_send, recv_sem=pair_recv.at[r, lin(pos)],
            device_id=other, device_id_type=MESH)

    def load(r, pos, kind):
        start, size = BACK[r]
        return pltpu.make_async_copy(
            partial.at[index_of(pos, core), pl.ds(start, size)], mine.at[lin(pos), pl.ds(start, size)],
            load_sem.at[kind])

    def prepare(r, pos):
        pair(r, pos).wait_recv()
        start, size = BACK[r]
        rows = pl.ds(start, size)
        mine[lin(pos), rows, :] = mine[lin(pos), rows, :] + theirs[lin(pos), rows, :]

    def slot(r, pos, phase):
        a = [pos[k] for k in ORDER[r]]
        return (20, 16 + a[0], a[0] * 4 + a[1])[phase]

    def hop(r, pos, phase, kind, d):
        half = None if kind else (0 if d == 1 else 1)
        start, size = rows_of(BACK, r, half)
        s = slot(r, pos, phase)
        lane = 2 if kind == 0 else (0 if d == 1 else 1)
        sem = (0 if d == 1 else 1) + 2 * kind
        return pltpu.make_async_remote_copy(
            src_ref=mine.at[lin(pos), pl.ds(start, size)],
            dst_ref=land.at[r, s * 3 + lane, pl.ds(start - BACK[r][0], size)],
            send_sem=send_sem, recv_sem=recv_sem.at[r, s, sem],
            device_id=dev_of(moved(me, ORDER[r][phase], d), core), device_id_type=MESH)

    def add(r, pos, phase, kind, d):
        hop(r, pos, phase, kind, d).wait_recv()
        half = None if kind else (0 if d == 1 else 1)
        start, size = rows_of(BACK, r, half)
        lane = 2 if kind == 0 else (0 if d == 1 else 1)
        rows = pl.ds(start, size)
        mine[lin(pos), rows, :] = (mine[lin(pos), rows, :]
                                   + land[r, slot(r, pos, phase) * 3 + lane, pl.ds(start - BACK[r][0], size), :])

    def far(r, base, phase):
        pos = moved(base, ORDER[r][phase], 2)
        if phase == 2:
            prepare(r, pos)
        for d in (1, -1):
            hop(r, pos, phase, 0, d).start()

    def near(r, base, phase):
        for d in (1, -1):
            pos = moved(base, ORDER[r][phase], d)
            if phase == 2:
                prepare(r, pos)
            add(r, pos, phase, 0, d)
            hop(r, pos, phase, 1, d).start()

    def here(r, base, phase):
        if phase == 2:
            prepare(r, base)
        for d in (1, -1):
            add(r, base, phase, 1, d)

    def order(i):
        return 2 + i

    def plane_base(r, i):
        return moved(moved(me, ORDER[r][0], order(i // 4)), ORDER[r][1], order(i % 4))

    def fetch(kind, offsets):
        def body(i, c):
            for r in range(3):
                for o in offsets:
                    pos = moved(plane_base(r, i), ORDER[r][2], o)
                    pair(r, pos).start()
                    load(r, pos, kind).start()
            return c
        return body

    for kind, offsets in enumerate(((2,), (1, -1), (0,))):
        lax.fori_loop(0, 16, fetch(kind, offsets), 0)
    for kind, step in enumerate((far, near, here)):
        loaded = mine.at[pl.ds(0, (16, 32, 16)[kind])]
        pltpu.make_async_copy(loaded, loaded, load_sem.at[kind]).wait()

        def plane(i, c, step=step):
            for r in range(3):
                step(r, plane_base(r, i), 2)
            return c
        lax.fori_loop(0, 16, plane, 0)
    for step in (far, near, here):
        def line(i, c, step=step):
            for r in range(3):
                step(r, moved(me, ORDER[r][0], order(i)), 1)
            return c
        lax.fori_loop(0, 4, line, 0)
    for step in (far, near, here):
        for r in range(3):
            step(r, me, 0)
    done = pltpu.make_async_copy(mine.at[lin(me)], out, out_sem)
    done.start()
    done.wait()
    pltpu.make_async_copy(theirs, theirs, pair_send).wait()
    most = theirs.at[pl.ds(0, 63)]
    pltpu.make_async_copy(most, most, send_sem).wait()


def scatter_all(partial):
    dma = pltpu.SemaphoreType.DMA
    rows = TILES * TOK
    return pl.pallas_call(
        scatter_kernel,
        out_shape=jax.ShapeDtypeStruct((rows, LANES), BF16),
        in_specs=[pl.BlockSpec(memory_space=pl.ANY)],
        out_specs=pl.BlockSpec(memory_space=pl.ANY),
        scratch_shapes=[pltpu.VMEM((64, rows, LANES), BF16), pltpu.VMEM((64, rows, LANES), BF16),
                        pltpu.VMEM((3, 63, 352, LANES), BF16),
                        dma, dma((3, 21, 4)), dma, dma((3, 64)), dma((3,)), dma],
        compiler_params=pltpu.CompilerParams(collective_id=1, has_side_effects=True, vmem_limit_bytes=60 * 1024 * 1024),
    )(partial)


def shards(tokens, out_grad, routes, gates, w_gate, w_up, w_down):
    y = lax.axis_index("mp")
    ids = jnp.arange(64, dtype=jnp.int32)
    named = jnp.sum((routes[:, :, None] == ids).astype(F32), axis=1)
    below = jnp.tril(jnp.ones((512, 512), F32), -1)
    before = jnp.dot(below.astype(BF16), named.astype(BF16), preferred_element_type=F32)
    before = jnp.sum(jnp.where(routes[:, :, None] == ids, before[:, None, :], 0.0), axis=2)
    own = lambda a: lax.dynamic_slice_in_dim(a, y * TOK, TOK, axis=0).T
    gate = own(gates)
    high = lax.reduce_precision(gate, 8, 7)
    meta = jnp.concatenate([own(routes).astype(F32), own(before), high, gate - high], axis=0).astype(BF16)
    tiled = lambda a: a.reshape(TOK, TILES, LANES).transpose(1, 0, 2)
    msg = jnp.concatenate([tiled(tokens), tiled(out_grad)], axis=1).reshape(META, LANES)
    msg = jnp.concatenate([msg, meta], axis=0)
    buf = gather_all(msg)
    partial, grad_gate, grad_up, grad_down = experts(buf, w_gate, w_up, w_down)
    back = scatter_all(partial)
    grad_tokens = back.reshape(TILES, TOK, LANES).transpose(1, 0, 2).reshape(TOK, TILES * LANES)
    return grad_tokens, grad_gate, grad_up, grad_down


def solution(mesh):
    in_specs = (
        P(("expert", "mp"), None),
        P(("expert", "mp"), None),
        P("expert", None),
        P("expert", None),
        P("expert", None, "mp"),
        P("expert", None, "mp"),
        P("expert", "mp", None),
    )
    out_specs = (
        P(("expert", "mp"), None),
        P("expert", None, "mp"),
        P("expert", None, "mp"),
        P("expert", "mp", None),
    )
    return jax.shard_map(shards, mesh=mesh, in_specs=in_specs, out_specs=out_specs, check_vma=False)
```

time: 605 us -> 297 us (0.49)
  waiting for transfers between devices: 304 us -> 0 us
  Pallas kernels: 0 us -> 290 us
  local copies, waits for them, and re-layouts: 131 us -> 3.64 us
  matrix products: 76.7 us -> 0.36 us
  other arithmetic: 43 us -> 2.5 us
  starting transfers between devices: 31.3 us -> 0 us
  between operations: 14.2 us -> 0.72 us
    all_to_all x3 -> x0, waiting for transfers between devices: 302 us -> none  [the longest x1 123 us: shards(): lax.all_to_all(send_dy, 'expert', split_axis=0, concat_axis=0, tiled=True)]
    pallas_call x0 -> x3, Pallas kernels: none -> 290 us  [the longest x1 133 us: gather_all(): pl.pallas_call(gather_kernel, out_shape=jax.ShapeDtypeStruct((128, MROWS,...]
    gather x4 -> x0, local copies, waits for them, and re-layouts: 99.8 us -> none  [the longest x1 28.7 us: shards(): gate_pad[owner][:, None] * dy_pad[token_rows].astype(jnp.float32)]
    dot_general x8 -> x1, matrix products: 76.7 us -> 0.36 us  [shards(): jnp.dot(below.astype(BF16), named.astype(BF16), preferred_element_type=F32)]
    another operation x3 -> x0, other arithmetic: 19 us -> none
    all_to_all x3 -> x0, starting transfers between devices: 18.8 us -> none  [the longest x1 8.49 us: shards(): lax.all_to_all(send_x, 'expert', split_axis=0, concat_axis=0, tiled=True)]
    scatter x1 -> x0, local copies, waits for them, and re-layouts: 15.5 us -> none  [shards(): owner = jnp.full((experts * capacity,), route_count, jnp.int32).at[slot]....]
    reduce_scatter x1 -> x0, starting transfers between devices: 12.4 us -> none  [shards(): lax.psum_scatter(group_dx.astype(jnp.bfloat16), 'mp', scatter_dimension=0...]
  transfers between devices with their start and end apart: 6 -> 0, of which waited for: 3 -> 0; matrix products, arithmetic and copies ran while one was open for 24% -> 0% of each run, Pallas kernels for 0% -> 0%
where the time goes in v1:
time: 297 us
  Pallas kernels  290 us (98%)
  local copies, waits for them, and re-layouts  3.64 us (1%)
    pallas_call x1, Pallas kernels, gather_all(): pl.pallas_call(gather_kernel, out_shape=jax.ShapeDtypeStruct((128, MROWS,...  133 us
    pallas_call x1, Pallas kernels, scatter_all(): pl.pallas_call(scatter_kernel, out_shape=jax.ShapeDtypeStruct((rows, LANE...  82.7 us
    pallas_call x1, Pallas kernels, experts(): pl.pallas_call(expert_kernel, grid=(128 // n,), out_shape=(jax.ShapeDtype...  73.6 us

profile of v1, /device:TPU:0, one launch (start us, length us, event | category | flops | bytes accessed | tf_op | source)
XLA Modules:
  0.0 296.8 jit_solution(18296318785937319295)
XLA Ops:
  0.6 0.0 copy-start
  0.7 0.9 convert_reduce_fusion
  1.5 0.0 copy-start.2
  1.5 0.4 fusion
  1.9 0.9 select_reduce_fusion
  2.8 0.0 copy-done
  2.8 1.1 bitcast_bitcast_fusion
  3.9 0.7 constant_dynamic-update-slice_fusion.3
  4.7 0.0 copy-done.2
  4.7 0.0 copy-start.1
  4.7 0.8 copy-done.1
  5.5 133.3 %shard_map.102.buf = bf16[128,2080,128]{2,1,0:T(8,128)(2,1)} custom-call(bf16[2080,128]{1,0:T(8,128)(2,1)} %copy-done.1), custom_call_target="tpu_custom_call" | custom-call | tf_op jit(solution)/shard_map/pallas_call | solution.py:135
  138.8 73.6 %shard_map.103 = (bf16[128,1024,128]{2,1,0:T(8,128)(2,1)}, f32[2,1024,256]{2,1,0:T(8,128)}, f32[2,1024,256]{2,1,0:T(8,128)}, f32[2,256,1024]{2,1,0:T(8,128)}) custom-call(bf16[128,2080,128]{2,1,0:T(8,128)(2,1)} %shard_map.102.buf, bf16[2,1024,256]{2,1,0:T(8,128)(2,1)} %wg.1, bf16[2,1024,256]{2,1,0:T(8,128)(2,1)} %wu.1, bf16[2,256,1024]{2,1,0:T(8,128)(2,1)} %wd.1), custom_call_target="tpu_custom_call" | custom-call | tf_op jit(solution)/shard_map/pallas_call | solution.py:230
  212.4 82.7 %shard_map.104 = bf16[1024,128]{1,0:T(8,128)(2,1)} custom-call(bf16[128,1024,128]{2,1,0:T(8,128)(2,1)} %get-tuple-element.8.partial), custom_call_target="tpu_custom_call" | custom-call | tf_op jit(solution)/shard_map/pallas_call | solution.py:360
  295.0 1.7 copy.25
  (6 shorter events, 0.1 us)
Async XLA Ops:
  0.6 2.1 copy-start
  1.5 3.1 %copy-start.2 = (f32[512,8]{0,1:T(8,128)S(1)}, f32[512,8]{0,1:T(8,128)}, u32[]{:S(2)}) copy-start(f32[512,8]{0,1:T(8,128)} %param.10) | copy-start | bytes 49156
  4.7 0.8 copy-start.1

commit v2 on v1

v2 whole, which is shorter than its diff:
```python
import jax
import jax.numpy as jnp
from jax import lax
from jax.experimental import pallas as pl
from jax.experimental.pallas import tpu as pltpu
from jax.sharding import PartitionSpec as P

MESH = pl.DeviceIdType.MESH
BF16, F32 = jnp.bfloat16, jnp.float32
TOK, TILES, LANES = 128, 8, 128
CAP = 80
META = TILES * 2 * TOK
MROWS = META + 32
SPLIT = ((0, 688), (688, 688), (1376, 704))
BACK = ((0, 336), (336, 336), (672, 352))
ORDER = ((0, 1, 2), (1, 2, 0), (2, 0, 1))


def where_am_i():
    e = lax.axis_index("expert")
    return (e // 8, (e // 2) % 4, lax.axis_index("mp")), e % 2


def dev_of(pos, core):
    return ((pos[0] * 4 + pos[1]) * 2 + core, pos[2])


def index_of(pos, core):
    return ((pos[0] * 4 + pos[1]) * 2 + core) * 4 + pos[2]


def lin(pos):
    return (pos[0] * 4 + pos[1]) * 4 + pos[2]


def moved(pos, axis, by):
    p = list(pos)
    p[axis] = (p[axis] + by + 4) % 4
    return tuple(p)


def rows_of(split, r, half):
    start, size = split[r]
    low = (size // 32) * 16
    if half is None:
        return start, size
    return (start, low) if half == 0 else (start + low, size - low)


def greet(me, core):
    barrier = pltpu.get_barrier_semaphore()
    for axis in range(3):
        for d in (1, -1):
            pl.semaphore_signal(barrier, inc=1, device_id=dev_of(moved(me, axis, d), core), device_id_type=MESH)
    pl.semaphore_signal(barrier, inc=1, device_id=dev_of(me, 1 - core), device_id_type=MESH)
    pl.semaphore_wait(barrier, 7)


def tn(a, b):
    return lax.dot_general(a, b, (((0,), (0,)), ((), ())), preferred_element_type=F32)


def nt(a, b):
    return lax.dot_general(a, b, (((1,), (1,)), ((), ())), preferred_element_type=F32)


BLOCKS = 4
NEAR4 = (0, 1, 3, 2)
COL_Z = (0, 1, 3, 0, 0, 1, 3, 1, 3, 2, 0, 2, 1, 2, 3, 2)
COL_X = (0, 0, 0, 1, 3, 1, 1, 3, 3, 0, 2, 1, 2, 3, 2, 2)
AHEAD = 4
LOOK = 4


def entry(table, i):
    out = 0
    for k, v in enumerate(table):
        if v:
            out = out + jnp.where(i == k, v, 0)
    return out


def gather_kernel(msg, wg, wu, wd, buf, kept, given, gg, gu, gd, slab, xs, ss, ps, part, stage,
                  send_sem, recv_sem, pair_send, pair_recv, own_sem, load_sem, stage_sem, given_sem):
    me, core = where_am_i()
    other = dev_of(me, 1 - core)
    first = lax.axis_index("expert") * 2
    greet(me, core)
    own = pltpu.make_async_copy(msg, buf.at[index_of(me, core)], own_sem)
    own.start()

    def ring(r, pos, half, axis, d, mine=False):
        start, size = rows_of(SPLIT, r, half)
        idx = index_of(pos, core)
        src = msg if mine else buf.at[idx]
        return pltpu.make_async_remote_copy(
            src_ref=src.at[pl.ds(start, size)], dst_ref=buf.at[idx, pl.ds(start, size)],
            send_sem=send_sem, recv_sem=recv_sem.at[r, lin(pos), 0 if half is None else half],
            device_id=dev_of(moved(me, axis, d), core), device_id_type=MESH)

    def pair(r, pos, mine=False):
        start, size = SPLIT[r]
        idx = index_of(pos, core)
        src = msg if mine else buf.at[idx]
        pltpu.make_async_remote_copy(
            src_ref=src.at[pl.ds(start, size)], dst_ref=buf.at[idx, pl.ds(start, size)],
            send_sem=pair_send, recv_sem=pair_recv.at[pos[0] * 4 + pos[1]],
            device_id=other, device_id_type=MESH).start()

    def send_full(r, pos, phases, mine=False):
        for p in phases:
            for d in (1, -1):
                ring(r, pos, None, ORDER[r][p], d, mine).start()

    def forward(r, base, phase):
        axis = ORDER[r][phase]
        for d in (1, -1):
            ring(r, moved(base, axis, -d), 0 if d == 1 else 1, axis, d).start()

    def near(r, base, phase, later=(), onward=True):
        axis = ORDER[r][phase]
        for d in (1, -1):
            pos = moved(base, axis, -d)
            ring(r, pos, None, axis, d).wait_recv()
            if onward:
                ring(r, pos, 0 if d == 1 else 1, axis, d).start()
            pair(r, pos)
            send_full(r, pos, later)

    def far(r, base, phase, later=()):
        axis = ORDER[r][phase]
        pos = moved(base, axis, 2)
        for half in (0, 1):
            ring(r, pos, half, axis, 1).wait_recv()
        pair(r, pos)
        send_full(r, pos, later)

    def column(i):
        return moved(moved(me, 0, entry(COL_Z, i)), 1, entry(COL_X, i))

    def base_of(r, i):
        return moved(moved(me, 1 if r == 1 else 0, entry(NEAR4, i // 4)), 2, entry(NEAR4, i % 4))

    def issue(u):
        def whole():
            for r in (1, 2):
                send_full(r, base_of(r, u), (2,))

        def halves():
            for r in (1, 2):
                for k in range(2):
                    forward(r, base_of(r, 2 * (u - 16) + k), 2)
        if isinstance(u, int):
            whole()
        else:
            pl.when(u < 16)(whole)
            pl.when((u >= 16) & (u < 24))(halves)

    for r in range(3):
        send_full(r, me, (0, 1, 2), mine=True)
    for r in range(3):
        pair(r, me, mine=True)
    for r in range(3):
        near(r, me, 0, (1,))
    for r in range(3):
        far(r, me, 0, (1,))
    for i in (1, 2):
        send_full(0, column(i), (2,))

    def line(step):
        def body(i, c):
            for r in range(3):
                step(r, moved(me, ORDER[r][0], entry(NEAR4, i)), 1)
            return c
        return body
    lax.fori_loop(0, 4, line(near), 0)
    for u in (1, 2):
        issue(u)
    lax.fori_loop(0, 4, line(far), 0)

    gg[...] = jnp.zeros_like(gg)
    gu[...] = jnp.zeros_like(gu)
    gd[...] = jnp.zeros_like(gd)
    own.wait()

    for u in range(3, LOOK):
        issue(u)
    send_full(0, column(3), (2,))

    def along_y(i):
        near(0, column(i), 2)

        @pl.when(i + AHEAD < 16)
        def _():
            send_full(0, column(i + AHEAD), (2,))

    def unit(u):
        @pl.when(u < 16)
        def _():
            for r in (1, 2):
                near(r, base_of(r, u), 2, onward=False)

        @pl.when((u >= 16) & (u < 24))
        def _():
            for r in (1, 2):
                for k in range(2):
                    far(r, base_of(r, 2 * (u - 16) + k), 2)
        issue(u + LOOK)

    def start_up(i, c):
        unit(i)
        along_y(i)
        return c
    lax.fori_loop(0, 3, start_up, 0)

    slots = lax.broadcasted_iota(jnp.int32, (CAP, TOK), 0).astype(F32)

    def staged(k, at):
        to = pl.ds(pl.multiple_of(at * 4, 4), 4)
        mine = stage.at[pl.ds(pl.multiple_of(k * 8 + core * 4, 4), 4)]
        theirs = stage.at[pl.ds(pl.multiple_of(k * 8 + (1 - core) * 4, 4), 4)]
        return (pltpu.make_async_copy(mine, kept.at[to], stage_sem.at[k, 0]),
                pltpu.make_async_remote_copy(src_ref=theirs, dst_ref=given.at[to], send_sem=stage_sem.at[k, 1],
                                             recv_sem=given_sem, device_id=other, device_id_type=MESH))

    def stage_wait():
        for k in range(2):
            stay, go = staged(k, 0)
            stay.wait()
            go.wait_send()

    def pick(b, at):
        hots, gates = [[], []], [0.0, 0.0]
        for y in range(4):
            meta = slab[at + b * 4 + y, pl.ds(META, 32), :].astype(F32)
            for j in range(2):
                named = (meta[0:8] == (first + j).astype(F32)).astype(F32)
                where = jnp.sum(named * (meta[8:16] + 1.0), axis=0, keepdims=True) - 1.0
                gate = jnp.sum(named * (meta[16:24] + meta[24:32]), axis=0, keepdims=True)
                hot = (slots == where).astype(F32)
                hots[j].append(hot)
                gates[j] = gates[j] + jnp.sum(hot * gate, axis=1, keepdims=True)
        hot = jnp.concatenate([jnp.concatenate(h, axis=1) for h in hots], axis=0).astype(BF16)
        gate = jnp.concatenate(gates, axis=0)
        ps[b] = hot
        for t in range(0, TILES, 2):
            def cols(off):
                return jnp.concatenate([
                    jnp.concatenate([slab[at + b * 4 + y, pl.ds((t + u) * 2 * TOK + off, TOK), :] for u in range(2)], axis=1)
                    for y in range(4)], axis=0)
            x = jnp.dot(hot, cols(0), preferred_element_type=F32).astype(BF16)
            s = (gate * jnp.dot(hot, cols(TOK), preferred_element_type=F32)).astype(BF16)
            for j in range(2):
                rows = pl.ds(pl.multiple_of(b * CAP, 16), CAP)
                xs[j, rows, pl.ds(t * LANES, 2 * LANES)] = x[j * CAP:(j + 1) * CAP]
                ss[j, rows, pl.ds(t * LANES, 2 * LANES)] = s[j * CAP:(j + 1) * CAP]
        return at

    def place(b, c):
        hot = ps[b]
        rows = pl.ds(pl.multiple_of(b * CAP, 16), CAP)
        for t in range(0, TILES, 2):
            both = jnp.concatenate([part[j, rows, pl.ds(t * LANES, 2 * LANES)] for j in range(2)], axis=0)
            out = tn(hot, both).astype(BF16)
            for y in range(4):
                for u in range(2):
                    stage[b * 4 + y, pl.ds((t + u) * TOK, TOK), :] = out[y * TOK:(y + 1) * TOK, u * LANES:(u + 1) * LANES]
        return c

    def main(j):
        x, s = xs[j], ss[j]
        pre_gate = jnp.dot(x, wg[j], preferred_element_type=F32)
        pre_up = jnp.dot(x, wu[j], preferred_element_type=F32)
        d_hidden = nt(s, wd[j])
        sig = jax.nn.sigmoid(pre_gate)
        act = pre_gate * sig
        hidden = (act * pre_up).astype(BF16)
        d_up = (d_hidden * act).astype(BF16)
        d_gate = (d_hidden * pre_up * sig * (1.0 + pre_gate * (1.0 - sig))).astype(BF16)
        gd[j] += tn(hidden, s)
        gg[j] += tn(x, d_gate)
        gu[j] += tn(x, d_up)
        part[j] = (nt(d_gate, wg[j]) + nt(d_up, wu[j])).astype(BF16)

    def column_at(i):
        pos = column(i)
        return pos[0] * 4 + pos[1]

    def load(p, k):
        at = column_at(2 * p + k) * 8
        half = p % 2
        return pltpu.make_async_copy(buf.at[pl.ds(pl.multiple_of(at, 8), 8)],
                                     slab.at[pl.ds(pl.multiple_of(half * 16 + k * 8, 8), 8)], load_sem.at[half, k])

    def compute(p, c):
        live, ready = p < 8, p >= 1
        at = ((p + 1) % 2) * 16
        unit(3 * p + 3)

        @pl.when(ready)
        def _():
            load(p - 1, 0).wait()
            lax.fori_loop(0, 2, pick, at)

        @pl.when(p < 7)
        def _():
            along_y(2 * p + 3)
        unit(3 * p + 4)

        @pl.when(ready)
        def _():
            load(p - 1, 1).wait()
            lax.fori_loop(2, 4, pick, at)

        @pl.when(p < 6)
        def _():
            along_y(2 * p + 4)
        unit(3 * p + 5)

        @pl.when(ready)
        def _():
            main(0)

        @pl.when(live)
        def _():
            for k in range(2):
                far(0, column(2 * p + k), 2)

        @pl.when(ready)
        def _():
            main(1)

        @pl.when(live)
        def _():
            for k in range(2):
                zx = column_at(2 * p + k)
                theirs = buf.at[pl.ds(pl.multiple_of(zx * 8 + (1 - core) * 4, 4), 4)]
                pltpu.make_async_copy(theirs, theirs, pair_recv.at[zx]).wait()
                load(p, k).start()

        pl.when(p >= 2)(stage_wait)

        @pl.when(ready)
        def _():
            lax.fori_loop(0, BLOCKS, place, 0)
            for k in range(2):
                stay, go = staged(k, column_at(2 * (p - 1) + k))
                stay.start()
                go.start()
        return c

    lax.fori_loop(0, 9, compute, 0)
    stage_wait()
    pltpu.make_async_copy(given, given, given_sem).wait()
    half = buf.at[pl.ds(0, 64)]
    pltpu.make_async_copy(half, half, pair_send).wait()
    most = buf.at[pl.ds(0, 63)]
    pltpu.make_async_copy(most, most, send_sem).wait()


def gather_and_compute(msg, wg, wu, wd):
    dma = pltpu.SemaphoreType.DMA
    hbm, vmem = pl.BlockSpec(memory_space=pl.ANY), pl.BlockSpec(memory_space=pltpu.VMEM)
    g = jax.ShapeDtypeStruct(wg.shape, F32)
    d = jax.ShapeDtypeStruct(wd.shape, F32)
    half = jax.ShapeDtypeStruct((64, TILES * TOK, LANES), BF16)
    n = BLOCKS * 4
    rows = pltpu.VMEM((2, BLOCKS * CAP, 1024), BF16)
    return pl.pallas_call(
        gather_kernel,
        out_shape=(jax.ShapeDtypeStruct((128, MROWS, LANES), BF16), half, half, g, g, d),
        in_specs=[hbm, vmem, vmem, vmem],
        out_specs=(hbm, hbm, hbm, vmem, vmem, vmem),
        scratch_shapes=[pltpu.VMEM((2 * n, MROWS, LANES), BF16), rows, rows,
                        pltpu.VMEM((BLOCKS, 2 * CAP, 512), BF16), rows,
                        pltpu.VMEM((n, TILES * TOK, LANES), BF16),
                        dma, dma((3, 64, 2)), dma, dma((16,)), dma, dma((2, 2)), dma((2, 2)), dma],
        compiler_params=pltpu.CompilerParams(collective_id=0, has_side_effects=True, vmem_limit_bytes=60 * 1024 * 1024),
    )(msg, wg, wu, wd)


OFFSETS = ((2,), (1, -1), (0,))
EARLY = 4


def scatter_kernel(kept, given, out, mine, theirs, land, send_sem, recv_sem, load_sem, out_sem):
    me, core = where_am_i()
    greet(me, core)

    def prepare(r, pos):
        start, size = BACK[r]
        rows = pl.ds(start, size)
        mine[lin(pos), rows, :] = mine[lin(pos), rows, :] + theirs[lin(pos), rows, :]

    def slot(r, pos, phase):
        a = [pos[k] for k in ORDER[r]]
        return (20, 16 + a[0], a[0] * 4 + a[1])[phase]

    def hop(r, pos, phase, kind, d):
        half = None if kind else (0 if d == 1 else 1)
        start, size = rows_of(BACK, r, half)
        s = slot(r, pos, phase)
        lane = 2 if kind == 0 else (0 if d == 1 else 1)
        sem = (0 if d == 1 else 1) + 2 * kind
        return pltpu.make_async_remote_copy(
            src_ref=mine.at[lin(pos), pl.ds(start, size)],
            dst_ref=land.at[r, s * 3 + lane, pl.ds(start - BACK[r][0], size)],
            send_sem=send_sem, recv_sem=recv_sem.at[r, s, sem],
            device_id=dev_of(moved(me, ORDER[r][phase], d), core), device_id_type=MESH)

    def add(r, pos, phase, kind, d):
        hop(r, pos, phase, kind, d).wait_recv()
        half = None if kind else (0 if d == 1 else 1)
        start, size = rows_of(BACK, r, half)
        lane = 2 if kind == 0 else (0 if d == 1 else 1)
        rows = pl.ds(start, size)
        mine[lin(pos), rows, :] = (mine[lin(pos), rows, :]
                                   + land[r, slot(r, pos, phase) * 3 + lane, pl.ds(start - BACK[r][0], size), :])

    def far(r, base, phase):
        pos = moved(base, ORDER[r][phase], 2)
        if phase == 2:
            prepare(r, pos)
        for d in (1, -1):
            hop(r, pos, phase, 0, d).start()

    def near(r, base, phase):
        for d in (1, -1):
            pos = moved(base, ORDER[r][phase], d)
            if phase == 2:
                prepare(r, pos)
            add(r, pos, phase, 0, d)
            hop(r, pos, phase, 1, d).start()

    def here(r, base, phase):
        if phase == 2:
            prepare(r, base)
        for d in (1, -1):
            add(r, base, phase, 1, d)

    def order(i):
        return 2 + i

    def plane_base(r, i):
        return moved(moved(me, ORDER[r][0], order(i // 4)), ORDER[r][1], order(i % 4))

    def fetch(kind, i):
        for r in range(3):
            start, size = BACK[r]
            for o in OFFSETS[kind]:
                pos = moved(plane_base(r, i), ORDER[r][2], o)
                for src, dst in ((kept, mine), (given, theirs)):
                    pltpu.make_async_copy(src.at[lin(pos), pl.ds(start, size)], dst.at[lin(pos), pl.ds(start, size)],
                                          load_sem.at[kind, i]).start()

    def first(i, c):
        fetch(0, i)
        return c
    lax.fori_loop(0, EARLY, first, 0)
    for kind, step in enumerate((far, near, here)):
        def plane(i, c, kind=kind, step=step):
            n = 2 * len(OFFSETS[kind])
            pltpu.make_async_copy(mine.at[pl.ds(0, n)], mine.at[pl.ds(0, n)], load_sem.at[kind, i]).wait()
            for r in range(3):
                step(r, plane_base(r, i), 2)

            @pl.when(i + EARLY < 16)
            def _():
                fetch(kind, i + EARLY)
            if kind < 2:
                @pl.when(i + EARLY >= 16)
                def _():
                    fetch(kind + 1, i + EARLY - 16)
            return c
        lax.fori_loop(0, 16, plane, 0)
    for step in (far, near, here):
        def line(i, c, step=step):
            for r in range(3):
                step(r, moved(me, ORDER[r][0], order(i)), 1)
            return c
        lax.fori_loop(0, 4, line, 0)
    for step in (far, near, here):
        for r in range(3):
            step(r, me, 0)
    done = pltpu.make_async_copy(mine.at[lin(me)], out, out_sem)
    done.start()
    done.wait()
    most = theirs.at[pl.ds(0, 63)]
    pltpu.make_async_copy(most, most, send_sem).wait()


def scatter_all(kept, given):
    dma = pltpu.SemaphoreType.DMA
    rows = TILES * TOK
    return pl.pallas_call(
        scatter_kernel,
        out_shape=jax.ShapeDtypeStruct((rows, LANES), BF16),
        in_specs=[pl.BlockSpec(memory_space=pl.ANY)] * 2,
        out_specs=pl.BlockSpec(memory_space=pl.ANY),
        scratch_shapes=[pltpu.VMEM((64, rows, LANES), BF16), pltpu.VMEM((64, rows, LANES), BF16),
                        pltpu.VMEM((3, 63, 352, LANES), BF16),
                        dma, dma((3, 21, 4)), dma((3, 16)), dma],
        compiler_params=pltpu.CompilerParams(collective_id=1, has_side_effects=True, vmem_limit_bytes=60 * 1024 * 1024),
    )(kept, given)


def shards(tokens, out_grad, routes, gates, w_gate, w_up, w_down):
    y = lax.axis_index("mp")
    ids = jnp.arange(64, dtype=jnp.int32)
    named = jnp.sum((routes[:, :, None] == ids).astype(F32), axis=1)
    below = jnp.tril(jnp.ones((512, 512), F32), -1)
    before = jnp.dot(below.astype(BF16), named.astype(BF16), preferred_element_type=F32)
    before = jnp.sum(jnp.where(routes[:, :, None] == ids, before[:, None, :], 0.0), axis=2)
    own = lambda a: lax.dynamic_slice_in_dim(a, y * TOK, TOK, axis=0).T
    gate = own(gates)
    high = lax.reduce_precision(gate, 8, 7)
    meta = jnp.concatenate([own(routes).astype(F32), own(before), high, gate - high], axis=0).astype(BF16)
    tiled = lambda a: a.reshape(TOK, TILES, LANES).transpose(1, 0, 2)
    msg = jnp.concatenate([tiled(tokens), tiled(out_grad)], axis=1).reshape(META, LANES)
    msg = jnp.concatenate([msg, meta], axis=0)
    _, kept, given, grad_gate, grad_up, grad_down = gather_and_compute(msg, w_gate, w_up, w_down)
    back = scatter_all(kept, given)
    grad_tokens = back.reshape(TILES, TOK, LANES).transpose(1, 0, 2).reshape(TOK, TILES * LANES)
    return grad_tokens, grad_gate, grad_up, grad_down


def solution(mesh):
    in_specs = (
        P(("expert", "mp"), None),
        P(("expert", "mp"), None),
        P("expert", None),
        P("expert", None),
        P("expert", None, "mp"),
        P("expert", None, "mp"),
        P("expert", "mp", None),
    )
    out_specs = (
        P(("expert", "mp"), None),
        P("expert", None, "mp"),
        P("expert", None, "mp"),
        P("expert", "mp", None),
    )
    return jax.shard_map(shards, mesh=mesh, in_specs=in_specs, out_specs=out_specs, check_vma=False)
```

time: 297 us -> 262 us (0.88)
  Pallas kernels: 290 us -> 248 us
  local copies, waits for them, and re-layouts: 3.64 us -> 9.66 us
    pallas_call x2 -> x1, Pallas kernels: 207 us -> 169 us  [gather_and_compute(): pl.pallas_call(gather_kernel, out_shape=(jax.ShapeDtypeStruct((128, MROWS...]
    unnamed x8 -> x17, local copies, waits for them, and re-layouts: 0.85 us -> 6.87 us
    pallas_call x1, Pallas kernels: 82.7 us -> 79.5 us  [scatter_all(): pl.pallas_call(scatter_kernel, out_shape=jax.ShapeDtypeStruct((rows, LANE...]
where the time goes in v2:
time: 262 us
  Pallas kernels  248 us (95%)
  local copies, waits for them, and re-layouts  9.66 us (4%)
    pallas_call x1, Pallas kernels, gather_and_compute(): pl.pallas_call(gather_kernel, out_shape=(jax.ShapeDtypeStruct((128, MROWS...  169 us
    pallas_call x1, Pallas kernels, scatter_all(): pl.pallas_call(scatter_kernel, out_shape=jax.ShapeDtypeStruct((rows, LANE...  79.5 us
    unnamed x17, local copies, waits for them, and re-layouts  6.87 us

profile of v2, /device:TPU:0, one launch (start us, length us, event | category | flops | bytes accessed | tf_op | source)
XLA Modules:
  0.0 261.5 jit_solution(10701506431458311452)
XLA Ops:
  0.6 0.0 copy-start
  0.7 0.9 convert_reduce_fusion
  1.5 0.0 copy-start.5
  1.5 0.4 fusion
  1.9 0.9 select_reduce_fusion
  2.8 0.0 copy-done
  2.8 1.1 bitcast_bitcast_fusion
  3.9 0.7 constant_dynamic-update-slice_fusion.3
  4.7 0.0 copy-done.5
  4.7 0.0 copy-start.1
  4.7 0.8 copy-done.1
  5.5 168.8 %shard_map.102 = (bf16[128,2080,128]{2,1,0:T(8,128)(2,1)}, bf16[64,1024,128]{2,1,0:T(8,128)(2,1)}, bf16[64,1024,128]{2,1,0:T(8,128)(2,1)}, f32[2,1024,256]{2,1,0...) custom-call(bf16[2080,128]{1,0:T(8,128)(2,1)} %copy-done.1, bf16[2,1024,256]{2,1,0:T(8,128)(2,1)} %wg.1, ...), custom_call_target="tpu_custom_call" | custom-call | tf_op jit(solution)/shard_map/pallas_call | solution.py:369
  174.3 0.0 copy-start.4
  174.3 79.5 %shard_map.103 = bf16[1024,128]{1,0:T(8,128)(2,1)} custom-call(bf16[64,1024,128]{2,1,0:T(8,128)(2,1)} %get-tuple-element.9.kept, bf16[64,1024,128]{2,1,0:T(8,128)(2,1)} %get-tuple-element.10.given), custom_call_target="tpu_custom_call" | custom-call | tf_op jit(solution)/shard_map/pallas_call | solution.py:495
  253.8 1.7 copy.25
  255.5 0.0 copy-done.4
  255.5 0.0 copy-start.3
  255.5 1.3 copy.33
  256.9 1.0 copy-done.3
  257.9 0.0 copy-start.2
  257.9 1.3 copy.34
  259.2 1.0 copy-done.2
  260.2 1.3 copy.35
  (6 shorter events, 0.1 us)
Async XLA Ops:
  0.6 2.1 copy-start
  1.5 3.1 %copy-start.5 = (f32[512,8]{0,1:T(8,128)S(1)}, f32[512,8]{0,1:T(8,128)}, u32[]{:S(2)}) copy-start(f32[512,8]{0,1:T(8,128)} %param.10) | copy-start | bytes 49156
  4.7 0.8 copy-start.1
  174.3 81.3 %copy-start.4 = (f32[2,1024,256]{2,1,0:T(8,128)S(1)}, f32[2,1024,256]{2,1,0:T(8,128)}, u32[]{:S(2)}) copy-start(f32[2,1024,256]{2,1,0:T(8,128)} %get-tuple-element.21) | copy-start | bytes 6291460
  255.5 2.3 copy-start.3
  257.9 2.3 copy-start.2

commit v3 on v2

v3 whole, which is shorter than its diff:
```python
import functools

import jax
import jax.numpy as jnp
from jax import lax
from jax.experimental import pallas as pl
from jax.experimental.pallas import tpu as pltpu
from jax.sharding import PartitionSpec as P

MESH = pl.DeviceIdType.MESH
BF16, F32 = jnp.bfloat16, jnp.float32
TOK, TILES, LANES = 128, 8, 128
CAP = 80
META = TILES * 2 * TOK
MROWS = META + 32
SPLIT = ((0, 688), (688, 688), (1376, 704))
BACK = ((0, 336), (336, 336), (672, 352))
ORDER = ((0, 1, 2), (1, 2, 0), (2, 0, 1))


def where_am_i():
    e = lax.axis_index("expert")
    return (e // 8, (e // 2) % 4, lax.axis_index("mp")), e % 2


def dev_of(pos, core):
    return ((pos[0] * 4 + pos[1]) * 2 + core, pos[2])


def index_of(pos, core):
    return ((pos[0] * 4 + pos[1]) * 2 + core) * 4 + pos[2]


def lin(pos):
    return (pos[0] * 4 + pos[1]) * 4 + pos[2]


def moved(pos, axis, by):
    p = list(pos)
    p[axis] = (p[axis] + by + 4) % 4
    return tuple(p)


def rows_of(split, r, half):
    start, size = split[r]
    low = (size // 32) * 16
    if half is None:
        return start, size
    return (start, low) if half == 0 else (start + low, size - low)


def greet(me, core):
    barrier = pltpu.get_barrier_semaphore()
    for axis in range(3):
        for d in (1, -1):
            pl.semaphore_signal(barrier, inc=1, device_id=dev_of(moved(me, axis, d), core), device_id_type=MESH)
    pl.semaphore_signal(barrier, inc=1, device_id=dev_of(me, 1 - core), device_id_type=MESH)
    pl.semaphore_wait(barrier, 7)


def tn(a, b):
    return lax.dot_general(a, b, (((0,), (0,)), ((), ())), preferred_element_type=F32)


def nt(a, b):
    return lax.dot_general(a, b, (((1,), (1,)), ((), ())), preferred_element_type=F32)


BLOCKS = 4
NEAR4 = (0, 1, 3, 2)
COL_Z = (0, 1, 3, 0, 0, 1, 3, 1, 3, 2, 0, 2, 1, 2, 3, 2)
COL_X = (0, 0, 0, 1, 3, 1, 1, 3, 3, 0, 2, 1, 2, 3, 2, 2)
AHEAD = 2
LOOK = 4


def entry(table, i):
    out = 0
    for k, v in enumerate(table):
        if v:
            out = out + jnp.where(i == k, v, 0)
    return out


def gather_kernel(msg, wg, wu, wd, buf, kept, gx, gd, slab, rows, away, ps, part, back, acts, stage, wx, wxt, wdt,
                  send_sem, recv_sem, own_sem, load_sem, rows_send, rows_recv, part_send, part_recv, stage_sem):
    me, core = where_am_i()
    other = dev_of(me, 1 - core)
    expert = lax.axis_index("expert")
    firsts = (2 * expert, 2 * (expert + 1 - 2 * core))
    greet(me, core)
    own = pltpu.make_async_copy(msg, buf.at[index_of(me, core)], own_sem)
    own.start()

    def ring(r, pos, half, axis, d, mine=False):
        start, size = rows_of(SPLIT, r, half)
        idx = index_of(pos, core)
        src = msg if mine else buf.at[idx]
        return pltpu.make_async_remote_copy(
            src_ref=src.at[pl.ds(start, size)], dst_ref=buf.at[idx, pl.ds(start, size)],
            send_sem=send_sem, recv_sem=recv_sem.at[r, lin(pos), 0 if half is None else half],
            device_id=dev_of(moved(me, axis, d), core), device_id_type=MESH)

    def send_full(r, pos, phases, mine=False):
        for p in phases:
            for d in (1, -1):
                ring(r, pos, None, ORDER[r][p], d, mine).start()

    def forward(r, base, phase):
        axis = ORDER[r][phase]
        for d in (1, -1):
            ring(r, moved(base, axis, -d), 0 if d == 1 else 1, axis, d).start()

    def near(r, base, phase, later=(), onward=True):
        axis = ORDER[r][phase]
        for d in (1, -1):
            pos = moved(base, axis, -d)
            ring(r, pos, None, axis, d).wait_recv()
            if onward:
                ring(r, pos, 0 if d == 1 else 1, axis, d).start()
            send_full(r, pos, later)

    def far(r, base, phase, later=()):
        axis = ORDER[r][phase]
        pos = moved(base, axis, 2)
        for half in (0, 1):
            ring(r, pos, half, axis, 1).wait_recv()
        send_full(r, pos, later)

    def column(i):
        return moved(moved(me, 0, entry(COL_Z, i)), 1, entry(COL_X, i))

    def base_of(r, i):
        return moved(moved(me, 1 if r == 1 else 0, entry(NEAR4, i // 4)), 2, entry(NEAR4, i % 4))

    def issue(u):
        def whole():
            for r in (1, 2):
                send_full(r, base_of(r, u), (2,))

        def halves():
            for r in (1, 2):
                for k in range(2):
                    forward(r, base_of(r, 2 * (u - 16) + k), 2)
        if isinstance(u, int):
            whole()
        else:
            pl.when(u < 16)(whole)
            pl.when((u >= 16) & (u < 24))(halves)

    for r in range(3):
        send_full(r, me, (0, 1, 2), mine=True)
    gx[...] = jnp.zeros_like(gx)
    gd[...] = jnp.zeros_like(gd)
    wx[:, :, 0:256] = wg[...]
    wx[:, :, 256:512] = wu[...]
    for j in range(2):
        wxt[j, 0:256] = wg[j].T
        wxt[j, 256:512] = wu[j].T
        wdt[j] = wd[j].T
    for r in range(3):
        near(r, me, 0, (1,))
    for r in range(3):
        far(r, me, 0, (1,))
    for i in (1,):
        send_full(0, column(i), (2,))

    def line(step):
        def body(i, c):
            for r in range(3):
                step(r, moved(me, ORDER[r][0], entry(NEAR4, i)), 1)
            return c
        return body
    lax.fori_loop(0, 4, line(near), 0)
    for u in (1, 2):
        issue(u)
    lax.fori_loop(0, 4, line(far), 0)

    own.wait()

    for u in range(3, LOOK):
        issue(u)
    def along_y(i):
        near(0, column(i), 2)

        @pl.when(i + AHEAD < 16)
        def _():
            send_full(0, column(i + AHEAD), (2,))

    def unit(u):
        @pl.when(u < 16)
        def _():
            for r in (1, 2):
                near(r, base_of(r, u), 2, onward=False)

        @pl.when((u >= 16) & (u < 24))
        def _():
            for r in (1, 2):
                for k in range(2):
                    far(r, base_of(r, 2 * (u - 16) + k), 2)
        issue(u + LOOK)

    def start_up(i, c):
        unit(i)
        pl.when(i < AHEAD - 1)(functools.partial(along_y, i))
        return c
    lax.fori_loop(0, 3, start_up, 0)

    slots = lax.broadcasted_iota(jnp.int32, (CAP, TOK), 0).astype(F32)

    def staged(k, at):
        return pltpu.make_async_copy(stage.at[pl.ds(k * 4, 4)], kept.at[pl.ds(pl.multiple_of(at * 4, 4), 4)], stage_sem.at[k])

    def send_rows(p, k):
        return pltpu.make_async_remote_copy(
            src_ref=away.at[k], dst_ref=rows.at[p % 2, 2 * k + core], send_sem=rows_send.at[k], recv_sem=rows_recv.at[k],
            device_id=other, device_id_type=MESH)

    def send_part(k):
        return pltpu.make_async_remote_copy(
            src_ref=part.at[2 * k + 1 - core], dst_ref=back.at[k], send_sem=part_send.at[k], recv_sem=part_recv.at[k],
            device_id=other, device_id_type=MESH)

    def pick(p, k):
        half = p % 2
        at = half * 8 + k * 4
        hots, gates = [[] for _ in range(4)], [0.0] * 4
        for y in range(4):
            meta = slab[at + y, pl.ds(META, 32), :].astype(F32)
            for j in range(4):
                named = (meta[0:8] == (firsts[j // 2] + j % 2).astype(F32)).astype(F32)
                where = jnp.sum(named * (meta[8:16] + 1.0), axis=0, keepdims=True) - 1.0
                gate = jnp.sum(named * (meta[16:24] + meta[24:32]), axis=0, keepdims=True)
                hot = (slots == where).astype(F32)
                hots[j].append(hot)
                gates[j] = gates[j] + hot * gate
        hot = jnp.concatenate([jnp.concatenate(h, axis=1) for h in hots], axis=0)
        gate = jnp.sum(jnp.concatenate(gates, axis=0), axis=1, keepdims=True)
        ps[k] = hot.T.astype(BF16)
        hot = hot.astype(BF16)
        for t in range(0, TILES, 2):
            for a in range(2):
                cols = jnp.concatenate([
                    jnp.concatenate([slab[at + y, pl.ds((t + u) * 2 * TOK + a * TOK, TOK), :] for u in range(2)], axis=1)
                    for y in range(4)], axis=0)
                got = jnp.dot(hot, cols, preferred_element_type=F32)
                got = (gate * got if a else got).astype(BF16)
                for j in range(2):
                    rows[half, 2 * k + core, a, j, :, pl.ds(t * LANES, 2 * LANES)] = got[j * CAP:(j + 1) * CAP]
                    away[k, a, j, :, pl.ds(t * LANES, 2 * LANES)] = got[(2 + j) * CAP:(3 + j) * CAP]

    def main(p, j):
        half = p % 2
        x = rows[half, :, 0, j].reshape(BLOCKS * CAP, 1024)
        s = rows[half, :, 1, j].reshape(BLOCKS * CAP, 1024)
        pre = jnp.dot(x, wx[j], preferred_element_type=F32)
        pre_gate, pre_up = pre[:, 0:256], pre[:, 256:512]
        d_hidden = jnp.dot(s, wdt[j], preferred_element_type=F32)
        sig = jax.nn.sigmoid(pre_gate)
        act = pre_gate * sig
        hidden = (act * pre_up).astype(BF16)
        d_up = (d_hidden * act).astype(BF16)
        d_gate = (d_hidden * pre_up * sig * (1.0 + pre_gate * (1.0 - sig))).astype(BF16)
        acts[j, :, 0:256] = hidden
        both = jnp.concatenate([d_gate, d_up], axis=1)
        acts[j, :, 256:768] = both
        part[:, j] = jnp.dot(both, wxt[j], preferred_element_type=F32).astype(BF16).reshape(BLOCKS, CAP, 1024)

    def weights(p, j):
        half = p % 2
        x = rows[half, :, 0, j].reshape(BLOCKS * CAP, 1024)
        s = rows[half, :, 1, j].reshape(BLOCKS * CAP, 1024)
        gd[j] += tn(acts[j, :, 0:256], s)
        gx[j] += tn(x, acts[j, :, 256:768])

    def place(k):
        hot = ps[k]
        for t in range(0, TILES, 2):
            cols = pl.ds(t * LANES, 2 * LANES)
            every = jnp.concatenate([part[2 * k + core, j, :, cols] for j in range(2)]
                                    + [back[k, j, :, cols] for j in range(2)], axis=0)
            out = jnp.dot(hot, every, preferred_element_type=F32).astype(BF16)
            for y in range(4):
                for u in range(2):
                    stage[k * 4 + y, pl.ds((t + u) * TOK, TOK), :] = out[y * TOK:(y + 1) * TOK, u * LANES:(u + 1) * LANES]

    def column_at(i):
        pos = column(i)
        return pos[0] * 4 + pos[1]

    def load(p, k):
        at = pl.multiple_of(column_at(2 * p + k) * 8 + core * 4, 4)
        half = p % 2
        return pltpu.make_async_copy(buf.at[pl.ds(at, 4)], slab.at[pl.ds(pl.multiple_of(half * 8 + k * 4, 4), 4)],
                                     load_sem.at[half, k])

    def compute(p, c):
        live, ready = p < 8, (p >= 1) & (p < 9)
        u = jnp.where(p < 5, 3 * p + 3, 2 * p + 8)
        unit(u)

        def picked(k):
            load(p - 1, k).wait()

            @pl.when(p >= 2)
            def _():
                send_rows(p, k).wait_send()
            pick(p - 1, k)
            send_rows(p - 1, k).start()
        pl.when(ready)(functools.partial(picked, 0))

        @pl.when(2 * p + AHEAD - 1 < 16)
        def _():
            along_y(2 * p + AHEAD - 1)
        unit(u + 1)
        pl.when(ready)(functools.partial(picked, 1))

        @pl.when(p >= 2)
        def _():
            for j in range(2):
                weights(p - 2, j)

        @pl.when(2 * p + AHEAD < 16)
        def _():
            along_y(2 * p + AHEAD)

        @pl.when(ready)
        def _():
            for k in range(2):
                send_rows(p - 1, k).wait_recv()

            @pl.when(p >= 2)
            def _():
                for k in range(2):
                    send_part(k).wait_send()
            for j in range(2):
                main(p - 1, j)
            for k in range(2):
                send_part(k).start()
        pl.when(p < 5)(lambda: unit(u + 2))

        @pl.when(live)
        def _():
            for k in range(2):
                far(0, column(2 * p + k), 2)
                load(p, k).start()

        @pl.when(ready)
        def _():
            @pl.when(p >= 2)
            def _():
                for k in range(2):
                    staged(k, 0).wait()
            for k in range(2):
                send_part(k).wait_recv()
                place(k)
                staged(k, column_at(2 * (p - 1) + k)).start()
        return c

    lax.fori_loop(0, 10, compute, 0)
    for k in range(2):
        staged(k, 0).wait()
        send_rows(0, k).wait_send()
        send_part(k).wait_send()
    most = buf.at[pl.ds(0, 63)]
    pltpu.make_async_copy(most, most, send_sem).wait()


def gather_and_compute(msg, wg, wu, wd):
    dma = pltpu.SemaphoreType.DMA
    hbm, vmem = pl.BlockSpec(memory_space=pl.ANY), pl.BlockSpec(memory_space=pltpu.VMEM)
    g = jax.ShapeDtypeStruct((2, 1024, 512), F32)
    d = jax.ShapeDtypeStruct(wd.shape, F32)
    bf = lambda *shape: pltpu.VMEM(shape, BF16)
    return pl.pallas_call(
        gather_kernel,
        out_shape=(jax.ShapeDtypeStruct((128, MROWS, LANES), BF16),
                   jax.ShapeDtypeStruct((64, TILES * TOK, LANES), BF16), g, d),
        in_specs=[vmem, vmem, vmem, vmem],
        out_specs=(hbm, hbm, vmem, vmem),
        scratch_shapes=[bf(16, MROWS, LANES), bf(2, BLOCKS, 2, 2, CAP, 1024), bf(2, 2, 2, CAP, 1024), bf(2, 512, 4 * CAP),
                        bf(BLOCKS, 2, CAP, 1024), bf(2, 2, CAP, 1024), bf(2, BLOCKS * CAP, 768), bf(8, TILES * TOK, LANES), bf(2, 1024, 512), bf(2, 512, 1024), bf(2, 1024, 256),
                        dma, dma((3, 64, 2)), dma, dma((2, 2)), dma((2,)), dma((2,)), dma((2,)), dma((2,)), dma((2,))],
        compiler_params=pltpu.CompilerParams(collective_id=0, has_side_effects=True, vmem_limit_bytes=60 * 1024 * 1024),
    )(msg, wg, wu, wd)


OFFSETS = ((2,), (1, -1), (0,))
EARLY = 4
LAG = 2
FAR4 = (2, 1, 3, 0)


def scatter_kernel(kept, out, mine, land, send_sem, recv_sem, load_sem, out_sem):
    me, core = where_am_i()
    greet(me, core)

    def slot(r, pos, phase):
        a = [pos[k] for k in ORDER[r]]
        return (20, 16 + a[0], a[0] * 4 + a[1])[phase]

    def hop(r, pos, phase, kind, d):
        half = None if kind else (0 if d == 1 else 1)
        start, size = rows_of(BACK, r, half)
        s = slot(r, pos, phase)
        lane = 2 if kind == 0 else (0 if d == 1 else 1)
        sem = (0 if d == 1 else 1) + 2 * kind
        return pltpu.make_async_remote_copy(
            src_ref=mine.at[lin(pos), pl.ds(start, size)],
            dst_ref=land.at[r, s * 3 + lane, pl.ds(start - BACK[r][0], size)],
            send_sem=send_sem, recv_sem=recv_sem.at[r, s, sem],
            device_id=dev_of(moved(me, ORDER[r][phase], d), core), device_id_type=MESH)

    def add(r, pos, phase, kind, d):
        hop(r, pos, phase, kind, d).wait_recv()
        half = None if kind else (0 if d == 1 else 1)
        start, size = rows_of(BACK, r, half)
        lane = 2 if kind == 0 else (0 if d == 1 else 1)
        rows = pl.ds(start, size)
        mine[lin(pos), rows, :] = (mine[lin(pos), rows, :]
                                   + land[r, slot(r, pos, phase) * 3 + lane, pl.ds(start - BACK[r][0], size), :])

    def far(r, base, phase):
        pos = moved(base, ORDER[r][phase], 2)
        for d in (1, -1):
            hop(r, pos, phase, 0, d).start()

    def near(r, base, phase):
        for d in (1, -1):
            pos = moved(base, ORDER[r][phase], d)
            add(r, pos, phase, 0, d)
            hop(r, pos, phase, 1, d).start()

    def here(r, base, phase):
        for d in (1, -1):
            add(r, base, phase, 1, d)

    def plane_base(r, i):
        return moved(moved(me, ORDER[r][0], entry(FAR4, i // 4)), ORDER[r][1], entry(FAR4, i % 4))

    def lines(step, l):
        for r in range(3):
            step(r, moved(me, ORDER[r][0], entry(FAR4, l)), 1)

    def ends(step):
        for r in range(3):
            step(r, me, 0)

    def fetch(kind, i):
        for r in range(3):
            start, size = BACK[r]
            for o in OFFSETS[kind]:
                pos = moved(plane_base(r, i), ORDER[r][2], o)
                pltpu.make_async_copy(kept.at[lin(pos), pl.ds(start, size)], mine.at[lin(pos), pl.ds(start, size)],
                                      load_sem.at[kind, i]).start()

    for kind in range(3):
        for i in range(EARLY - kind * LAG):
            fetch(kind, i)

    def plane(i, c):
        for kind, step in enumerate((far, near, here)):
            k = i - kind * LAG

            @pl.when((k + EARLY < 16) & (k + EARLY >= 0))
            def _(kind=kind, k=k):
                fetch(kind, k + EARLY)
        for kind, step in enumerate((far, near, here)):
            k = i - kind * LAG

            @pl.when((k >= 0) & (k < 16))
            def _(kind=kind, k=k, step=step):
                n = len(OFFSETS[kind])
                pltpu.make_async_copy(mine.at[pl.ds(0, n)], mine.at[pl.ds(0, n)], load_sem.at[kind, k]).wait()
                for r in range(3):
                    step(r, plane_base(r, k), 2)
        k = i - 2 * LAG
        for l in range(4):
            @pl.when(k == 4 * l + 3)
            def _(l=l):
                lines(far, l)
                if l >= 1:
                    lines(near, l - 1)
                if l >= 2:
                    lines(here, l - 2)
                if l == 2:
                    ends(far)
        return c
    lax.fori_loop(0, 16 + 2 * LAG, plane, 0)
    lines(here, 2)
    ends(near)
    lines(near, 3)
    lines(here, 3)
    ends(here)
    done = pltpu.make_async_copy(mine.at[lin(me)], out, out_sem)
    done.start()
    done.wait()
    most = mine.at[pl.ds(0, 63)]
    pltpu.make_async_copy(most, most, send_sem).wait()


def scatter_all(kept):
    dma = pltpu.SemaphoreType.DMA
    rows = TILES * TOK
    return pl.pallas_call(
        scatter_kernel,
        out_shape=jax.ShapeDtypeStruct((rows, LANES), BF16),
        in_specs=[pl.BlockSpec(memory_space=pl.ANY)],
        out_specs=pl.BlockSpec(memory_space=pl.ANY),
        scratch_shapes=[pltpu.VMEM((64, rows, LANES), BF16),
                        pltpu.VMEM((3, 63, 352, LANES), BF16),
                        dma, dma((3, 21, 4)), dma((3, 16)), dma],
        compiler_params=pltpu.CompilerParams(collective_id=1, has_side_effects=True, vmem_limit_bytes=60 * 1024 * 1024),
    )(kept)


def shards(tokens, out_grad, routes, gates, w_gate, w_up, w_down):
    y = lax.axis_index("mp")
    ids = jnp.arange(64, dtype=jnp.int32)
    named = jnp.sum((routes[:, :, None] == ids).astype(F32), axis=1)
    below = jnp.tril(jnp.ones((512, 512), F32), -1)
    before = jnp.dot(below.astype(BF16), named.astype(BF16), preferred_element_type=F32)
    before = jnp.sum(jnp.where(routes[:, :, None] == ids, before[:, None, :], 0.0), axis=2)
    own = lambda a: lax.dynamic_slice_in_dim(a, y * TOK, TOK, axis=0).T
    gate = own(gates)
    high = lax.reduce_precision(gate, 8, 7)
    meta = jnp.concatenate([own(routes).astype(F32), own(before), high, gate - high], axis=0).astype(BF16)
    tiled = lambda a: a.reshape(TOK, TILES, LANES).transpose(1, 0, 2)
    msg = jnp.concatenate([tiled(tokens), tiled(out_grad)], axis=1).reshape(META, LANES)
    msg = jnp.concatenate([msg, meta], axis=0)
    _, kept, both, grad_down = gather_and_compute(msg, w_gate, w_up, w_down)
    grad_gate, grad_up = both[:, :, 0:256], both[:, :, 256:512]
    back = scatter_all(kept)
    grad_tokens = back.reshape(TILES, TOK, LANES).transpose(1, 0, 2).reshape(TOK, TILES * LANES)
    return grad_tokens, grad_gate, grad_up, grad_down


def solution(mesh):
    in_specs = (
        P(("expert", "mp"), None),
        P(("expert", "mp"), None),
        P("expert", None),
        P("expert", None),
        P("expert", None, "mp"),
        P("expert", None, "mp"),
        P("expert", "mp", None),
    )
    out_specs = (
        P(("expert", "mp"), None),
        P("expert", None, "mp"),
        P("expert", None, "mp"),
        P("expert", "mp", None),
    )
    return jax.shard_map(shards, mesh=mesh, in_specs=in_specs, out_specs=out_specs, check_vma=False)
```

time: 262 us -> 250 us (0.954)
  Pallas kernels: 248 us -> 237 us
    pallas_call x1, Pallas kernels: 79.5 us -> 73.5 us  [scatter_all(): pl.pallas_call(scatter_kernel, out_shape=jax.ShapeDtypeStruct((rows, LANE...]
    pallas_call x1, Pallas kernels: 169 us -> 163 us  [gather_and_compute(): pl.pallas_call(gather_kernel, out_shape=(jax.ShapeDtypeStruct((128, MROWS...]
    slice x0 -> x1, local copies, waits for them, and re-layouts: none -> 4.75 us  [shards(): grad_gate, grad_up = (both[:, :, 0:256], both[:, :, 256:512])]
    unnamed x17 -> x11, local copies, waits for them, and re-layouts: 6.87 us -> 2.17 us
where the time goes in v3:
time: 250 us
  Pallas kernels  237 us (95%)
  local copies, waits for them, and re-layouts  9.72 us (4%)
  other arithmetic  2.5 us (1%)
    pallas_call x1, Pallas kernels, gather_and_compute(): pl.pallas_call(gather_kernel, out_shape=(jax.ShapeDtypeStruct((128, MROWS...  163 us
    pallas_call x1, Pallas kernels, scatter_all(): pl.pallas_call(scatter_kernel, out_shape=jax.ShapeDtypeStruct((rows, LANE...  73.5 us

profile of v3, /device:TPU:0, one launch (start us, length us, event | category | flops | bytes accessed | tf_op | source)
XLA Modules:
  0.0 250.1 jit_solution(11750113810817145583)
XLA Ops:
  0.6 0.0 copy-start
  0.7 0.9 convert_reduce_fusion
  1.5 0.0 copy-start.3
  1.5 0.4 fusion
  1.9 0.9 select_reduce_fusion
  2.8 0.0 copy-done
  2.8 1.1 bitcast_bitcast_fusion
  3.9 0.7 constant_dynamic-update-slice_fusion.3
  4.7 0.0 copy-done.3
  4.7 0.0 copy-start.1
  4.7 0.8 copy-done.1
  5.5 163.3 %shard_map.102 = (bf16[128,2080,128]{2,1,0:T(8,128)(2,1)}, bf16[64,1024,128]{2,1,0:T(8,128)(2,1)}, f32[2,1024,512]{2,1,0:T(8,128)}, f32[2,256,1024]{2,1,0:T(8,128)}) custom-call(bf16[2080,128]{1,0:T(8,128)(2,1)} %copy-done.1, bf16[2,1024,256]{2,1,0:T(8,128)(2,1)} %wg.1, bf16[2,1024,256]{2,1,0:T(8,128)(2,1)} %wu.1, bf16[2,256,1024]{2,1,0:T(8,128)(2,1)} %wd.1), custom_call_target="tpu_custom_call" | custom-call | tf_op jit(solution)/shard_map/pallas_call | solution.py:375
  168.8 73.5 %shard_map.103 = bf16[1024,128]{1,0:T(8,128)(2,1)} custom-call(bf16[64,1024,128]{2,1,0:T(8,128)(2,1)} %get-tuple-element.7.kept), custom_call_target="tpu_custom_call" | custom-call | tf_op jit(solution)/shard_map/pallas_call | solution.py:505
  242.3 1.7 copy.25
  244.0 0.0 copy-start.2
  244.0 4.7 %fusion.10 = (f32[2,1024,256]{2,1,0:T(8,128)}, f32[2,1024,256]{2,1,0:T(8,128)}) fusion(f32[2,1024,512]{2,1,0:T(8,128)} %get-tuple-element.8), kind=kLoop, calls=%fused_computation.29 | loop fusion | bytes 8388608 | tf_op jit(solution)/shard_map/slice | solution.py:532
  248.8 0.0 copy-done.2
  248.8 1.3 copy.31
  (6 shorter events, 0.1 us)
Async XLA Ops:
  0.6 2.1 copy-start
  1.5 3.1 %copy-start.3 = (f32[512,8]{0,1:T(8,128)S(1)}, f32[512,8]{0,1:T(8,128)}, u32[]{:S(2)}) copy-start(f32[512,8]{0,1:T(8,128)} %param.10) | copy-start | bytes 49156
  4.7 0.8 copy-start.1
  244.0 4.8 %copy-start.2 = (f32[2,256,1024]{2,1,0:T(8,128)S(1)}, f32[2,256,1024]{2,1,0:T(8,128)}, u32[]{:S(2)}) copy-start(f32[2,256,1024]{2,1,0:T(8,128)} %get-tuple-element.21) | copy-start | bytes 6291460

commit v4 on v3

--- a/solution.py
+++ b/solution.py
@@ -514,6 +514,33 @@
     )(kept)
 
 
+PIECES = 2
+
+
+def write_kernel(both, down, back, tokens_out, gate_out, up_out, down_out):
+    @pl.when(pl.program_id(0) == 0)
+    def _():
+        for t in range(TILES):
+            tokens_out[:, t * LANES:(t + 1) * LANES] = back[t * TOK:(t + 1) * TOK, :]
+    gate_out[...] = both[:, :, 0:256]
+    up_out[...] = both[:, :, 256:512]
+    down_out[...] = down[...]
+
+
+def write_all(both, down, back):
+    piece = lambda r, c: pl.BlockSpec((1, r // PIECES, c), lambda i: (i // PIECES, i % PIECES, 0))
+    whole = lambda *shape: pl.BlockSpec(shape, lambda i: (0, 0))
+    return pl.pallas_call(
+        write_kernel,
+        grid=(2 * PIECES,),
+        out_shape=(jax.ShapeDtypeStruct((TOK, TILES * LANES), BF16), jax.ShapeDtypeStruct((2, 1024, 256), F32),
+                   jax.ShapeDtypeStruct((2, 1024, 256), F32), jax.ShapeDtypeStruct((2, 256, 1024), F32)),
+        in_specs=[piece(1024, 512), piece(256, 1024), whole(TILES * TOK, LANES)],
+        out_specs=(whole(TOK, TILES * LANES), piece(1024, 256), piece(1024, 256), piece(256, 1024)),
+        compiler_params=pltpu.CompilerParams(vmem_limit_bytes=32 * 1024 * 1024),
+    )(both, down, back)
+
+
 def shards(tokens, out_grad, routes, gates, w_gate, w_up, w_down):
     y = lax.axis_index("mp")
     ids = jnp.arange(64, dtype=jnp.int32)
@@ -529,10 +556,7 @@
     msg = jnp.concatenate([tiled(tokens), tiled(out_grad)], axis=1).reshape(META, LANES)
     msg = jnp.concatenate([msg, meta], axis=0)
     _, kept, both, grad_down = gather_and_compute(msg, w_gate, w_up, w_down)
-    grad_gate, grad_up = both[:, :, 0:256], both[:, :, 256:512]
-    back = scatter_all(kept)
-    grad_tokens = back.reshape(TILES, TOK, LANES).transpose(1, 0, 2).reshape(TOK, TILES * LANES)
-    return grad_tokens, grad_gate, grad_up, grad_down
+    return write_all(both, grad_down, scatter_all(kept))
 
 
 def solution(mesh):

time: 250 us -> 249 us (level)
  local copies, waits for them, and re-layouts: 9.72 us -> 5.06 us
  Pallas kernels: 237 us -> 240 us
    slice x1 -> x0, local copies, waits for them, and re-layouts: 4.75 us -> none  [shards(): grad_gate, grad_up = (both[:, :, 0:256], both[:, :, 256:512])]
    pallas_call x0 -> x1, Pallas kernels: none -> 3.11 us  [write_all(): pl.pallas_call(write_kernel, grid=(2 * PIECES,), out_shape=(jax.ShapeDtyp...]
where the time goes in v4:
time: 249 us
  Pallas kernels  240 us (96%)
  local copies, waits for them, and re-layouts  5.06 us (2%)
  other arithmetic  2.5 us (1%)
    pallas_call x1, Pallas kernels, gather_and_compute(): pl.pallas_call(gather_kernel, out_shape=(jax.ShapeDtypeStruct((128, MROWS...  163 us
    pallas_call x1, Pallas kernels, scatter_all(): pl.pallas_call(scatter_kernel, out_shape=jax.ShapeDtypeStruct((rows, LANE...  73.5 us

profile of v4, /device:TPU:0, one launch (start us, length us, event | category | flops | bytes accessed | tf_op | source)
XLA Modules:
  0.0 248.6 jit_solution(4082766794574142052)
XLA Ops:
  0.6 0.0 copy-start
  0.7 0.9 convert_reduce_fusion
  1.5 0.0 copy-start.5
  1.5 0.4 fusion
  1.9 0.9 select_reduce_fusion
  2.8 0.0 copy-done
  2.8 1.1 bitcast_bitcast_fusion
  3.9 0.7 constant_dynamic-update-slice_fusion.3
  4.7 0.0 copy-done.5
  4.7 0.0 copy-start.4
  4.7 0.8 copy-done.4
  5.5 163.3 %shard_map.102 = (bf16[128,2080,128]{2,1,0:T(8,128)(2,1)}, bf16[64,1024,128]{2,1,0:T(8,128)(2,1)}, f32[2,1024,512]{2,1,0:T(8,128)}, f32[2,256,1024]{2,1,0:T(8,128)}) custom-call(bf16[2080,128]{1,0:T(8,128)(2,1)} %copy-done.4, bf16[2,1024,256]{2,1,0:T(8,128)(2,1)} %wg.1, bf16[2,1024,256]{2,1,0:T(8,128)(2,1)} %wu.1, bf16[2,256,1024]{2,1,0:T(8,128)(2,1)} %wd.1), custom_call_target="tpu_custom_call" | custom-call | tf_op jit(solution)/shard_map/pallas_call | solution.py:375
  168.8 0.0 copy-start.2
  168.8 73.5 %shard_map.103.back = bf16[1024,128]{1,0:T(8,128)(2,1)} custom-call(bf16[64,1024,128]{2,1,0:T(8,128)(2,1)} %get-tuple-element.9.kept), custom_call_target="tpu_custom_call" | custom-call | tf_op jit(solution)/shard_map/pallas_call | solution.py:505
  242.3 0.0 copy-done.2
  242.3 0.0 copy-start.1
  242.3 2.2 copy-done.1
  244.5 0.0 copy-start.3
  244.5 0.9 copy-done.3
  245.5 3.1 %shard_map.104 = (bf16[128,1024]{1,0:T(8,128)(2,1)}, f32[2,1024,256]{2,1,0:T(8,128)}, f32[2,1024,256]{2,1,0:T(8,128)}, f32[2,256,1024]{2,1,0:T(8,128)}) custom-call(f32[2,1024,512]{2,1,0:T(8,128)S(1)} %copy-done.1, f32[2,256,1024]{2,1,0:T(8,128)S(1)} %copy-done.2, bf16[1024,128]{1,0:T(8,128)(2,1)S(1)} %copy-done.3), custom_call_target="tpu_custom_call" | custom-call | tf_op jit(solution)/shard_map/pallas_call | solution.py:533
  (6 shorter events, 0.1 us)
Async XLA Ops:
  0.6 2.1 copy-start
  1.5 3.1 %copy-start.5 = (f32[512,8]{0,1:T(8,128)S(1)}, f32[512,8]{0,1:T(8,128)}, u32[]{:S(2)}) copy-start(f32[512,8]{0,1:T(8,128)} %param.10) | copy-start | bytes 49156
  4.7 0.8 copy-start.4
  168.8 73.5 %copy-start.2 = (f32[2,256,1024]{2,1,0:T(8,128)S(1)}, f32[2,256,1024]{2,1,0:T(8,128)}, u32[]{:S(2)}) copy-start(f32[2,256,1024]{2,1,0:T(8,128)} %get-tuple-element.8.down) | copy-start | bytes 6291460
  242.3 2.2 copy-start.1
  244.5 0.9 copy-start.3

commit v5 on v4

--- a/solution.py
+++ b/solution.py
@@ -82,12 +82,21 @@
     return out
 
 
-def gather_kernel(msg, wg, wu, wd, buf, kept, gx, gd, slab, rows, away, ps, part, back, acts, stage, wx, wxt, wdt,
+def gather_kernel(x_in, dy_in, meta_in, wg_in, wu_in, wd_in, buf, kept, gx, gd, slab, rows, away, ps, part, back, acts, stage, wx, wxt, wdt, msg, wg, wu, wd, w_sem,
                   send_sem, recv_sem, own_sem, load_sem, rows_send, rows_recv, part_send, part_recv, stage_sem):
     me, core = where_am_i()
     other = dev_of(me, 1 - core)
     expert = lax.axis_index("expert")
     firsts = (2 * expert, 2 * (expert + 1 - 2 * core))
+    weights_in = [pltpu.make_async_copy(src, dst, w_sem.at[i])
+                  for i, (src, dst) in enumerate(((wg_in, wg), (wu_in, wu), (wd_in, wd)))]
+    for copy in weights_in:
+        copy.start()
+    for t in range(TILES):
+        cols = slice(t * LANES, (t + 1) * LANES)
+        msg[2 * t * TOK:(2 * t + 1) * TOK, :] = x_in[:, cols]
+        msg[(2 * t + 1) * TOK:(2 * t + 2) * TOK, :] = dy_in[:, cols]
+    msg[META:MROWS, :] = meta_in[...]
     greet(me, core)
     own = pltpu.make_async_copy(msg, buf.at[index_of(me, core)], own_sem)
     own.start()
@@ -152,6 +161,8 @@
         send_full(r, me, (0, 1, 2), mine=True)
     gx[...] = jnp.zeros_like(gx)
     gd[...] = jnp.zeros_like(gd)
+    for copy in weights_in:
+        copy.wait()
     wx[:, :, 0:256] = wg[...]
     wx[:, :, 256:512] = wu[...]
     for j in range(2):
@@ -366,7 +377,7 @@
     pltpu.make_async_copy(most, most, send_sem).wait()
 
 
-def gather_and_compute(msg, wg, wu, wd):
+def gather_and_compute(x, dy, meta, wg, wu, wd):
     dma = pltpu.SemaphoreType.DMA
     hbm, vmem = pl.BlockSpec(memory_space=pl.ANY), pl.BlockSpec(memory_space=pltpu.VMEM)
     g = jax.ShapeDtypeStruct((2, 1024, 512), F32)
@@ -376,13 +387,14 @@
         gather_kernel,
         out_shape=(jax.ShapeDtypeStruct((128, MROWS, LANES), BF16),
                    jax.ShapeDtypeStruct((64, TILES * TOK, LANES), BF16), g, d),
-        in_specs=[vmem, vmem, vmem, vmem],
+        in_specs=[vmem] * 3 + [hbm] * 3,
         out_specs=(hbm, hbm, vmem, vmem),
         scratch_shapes=[bf(16, MROWS, LANES), bf(2, BLOCKS, 2, 2, CAP, 1024), bf(2, 2, 2, CAP, 1024), bf(2, 512, 4 * CAP),
-                        bf(BLOCKS, 2, CAP, 1024), bf(2, 2, CAP, 1024), bf(2, BLOCKS * CAP, 768), bf(8, TILES * TOK, LANES), bf(2, 1024, 512), bf(2, 512, 1024), bf(2, 1024, 256),
+                        bf(BLOCKS, 2, CAP, 1024), bf(2, 2, CAP, 1024), bf(2, BLOCKS * CAP, 768), bf(8, TILES * TOK, LANES), bf(2, 1024, 512), bf(2, 512, 1024), bf(2, 1024, 256), bf(MROWS, LANES),
+                        bf(2, 1024, 256), bf(2, 1024, 256), bf(2, 256, 1024), dma((3,)),
                         dma, dma((3, 64, 2)), dma, dma((2, 2)), dma((2,)), dma((2,)), dma((2,)), dma((2,)), dma((2,))],
         compiler_params=pltpu.CompilerParams(collective_id=0, has_side_effects=True, vmem_limit_bytes=60 * 1024 * 1024),
-    )(msg, wg, wu, wd)
+    )(x, dy, meta, wg, wu, wd)
 
 
 OFFSETS = ((2,), (1, -1), (0,))
@@ -552,10 +564,7 @@
     gate = own(gates)
     high = lax.reduce_precision(gate, 8, 7)
     meta = jnp.concatenate([own(routes).astype(F32), own(before), high, gate - high], axis=0).astype(BF16)
-    tiled = lambda a: a.reshape(TOK, TILES, LANES).transpose(1, 0, 2)
-    msg = jnp.concatenate([tiled(tokens), tiled(out_grad)], axis=1).reshape(META, LANES)
-    msg = jnp.concatenate([msg, meta], axis=0)
-    _, kept, both, grad_down = gather_and_compute(msg, w_gate, w_up, w_down)
+    _, kept, both, grad_down = gather_and_compute(tokens, out_grad, meta, w_gate, w_up, w_down)
     return write_all(both, grad_down, scatter_all(kept))
 
 

time: 249 us -> 247 us (level)
  no operation moved by 1% of the time
where the time goes in v5:
time: 247 us
  Pallas kernels  239 us (97%)
  other arithmetic  3.67 us (1%)
  local copies, waits for them, and re-layouts  3.14 us (1%)
    pallas_call x1, Pallas kernels, gather_and_compute(): pl.pallas_call(gather_kernel, out_shape=(jax.ShapeDtypeStruct((128, MROWS...  163 us
    pallas_call x1, Pallas kernels, scatter_all(): pl.pallas_call(scatter_kernel, out_shape=jax.ShapeDtypeStruct((rows, LANE...  73.6 us

profile of v5, /device:TPU:0, one launch (start us, length us, event | category | flops | bytes accessed | tf_op | source)
XLA Modules:
  0.0 247.1 jit_solution(2416455391458169151)
XLA Ops:
  0.6 0.7 fusion.6
  1.3 0.7 reduce-precision_convert_fusion
  2.0 0.8 convert_reduce_fusion
  2.9 0.4 fusion
  3.2 0.9 select_reduce_fusion
  4.1 0.6 pad_maximum_fusion.meta_in
  4.7 162.5 %shard_map.102 = (bf16[128,2080,128]{2,1,0:T(8,128)(2,1)}, bf16[64,1024,128]{2,1,0:T(8,128)(2,1)}, f32[2,1024,512]{2,1,0:T(8,128)}, f32[2,256,1024]{2,1,0:T(8,128)}) custom-call(bf16[128,1024]{1,0:T(8,128)(2,1)} %x_in.1, bf16[128,1024]{1,0:T(8,128)(2,1)} %dy_in.1, bf16[32,128]{1,0:T(8,128)(2,1)} %pad_maximum_fusion.meta_in, bf16[2,1024,256]{2,1,0:T(8,128)(2,1)} %wg_in.1, ...), custom_call_target="tpu_custom_call" | custom-call | tf_op jit(solution)/shard_map/pallas_call | solution.py:386
  167.2 0.0 copy-start.1
  167.2 73.6 %shard_map.103.back = bf16[1024,128]{1,0:T(8,128)(2,1)} custom-call(bf16[64,1024,128]{2,1,0:T(8,128)(2,1)} %get-tuple-element.9.kept), custom_call_target="tpu_custom_call" | custom-call | tf_op jit(solution)/shard_map/pallas_call | solution.py:517
  240.8 0.0 copy-done.1
  240.8 0.0 copy-start
  240.9 2.2 copy-done
  243.0 0.0 copy-start.2
  243.0 0.9 copy-done.2
  244.0 3.1 %shard_map.104 = (bf16[128,1024]{1,0:T(8,128)(2,1)}, f32[2,1024,256]{2,1,0:T(8,128)}, f32[2,1024,256]{2,1,0:T(8,128)}, f32[2,256,1024]{2,1,0:T(8,128)}) custom-call(f32[2,1024,512]{2,1,0:T(8,128)S(1)} %copy-done, f32[2,256,1024]{2,1,0:T(8,128)S(1)} %copy-done.1, bf16[1024,128]{1,0:T(8,128)(2,1)S(1)} %copy-done.2), custom_call_target="tpu_custom_call" | custom-call | tf_op jit(solution)/shard_map/pallas_call | solution.py:545
  (2 shorter events, 0.0 us)
Async XLA Ops:
  167.2 73.6 %copy-start.1 = (f32[2,256,1024]{2,1,0:T(8,128)S(1)}, f32[2,256,1024]{2,1,0:T(8,128)}, u32[]{:S(2)}) copy-start(f32[2,256,1024]{2,1,0:T(8,128)} %get-tuple-element.8.down) | copy-start | bytes 6291460
  240.8 2.2 copy-start
  243.0 0.9 copy-start.2
